TPU v7x, 512 devices: a whole 4x8x8 slice. The times are simulated.
512 devices in a mesh: ctx: 64 (over y, z), ch: 8 (over x, core).
Axes of the slice: x: 4, y: 8, z: 8, core: 2. Of those that a mesh axis runs over, the one named last changes fastest.
Arguments:
- inputs: bfloat16 [3, 1024, 16384], P(None, 'ch', 'ctx'), may hold values from -6 to 6
- short_weight: float32 [3, 1024, 7], P(None, 'ch'), may hold values from -2 to 2
- skip: float32 [1024], P('ch'), may hold values from -1 to 1
- filters: float32 [64, 16384], P('ch', 'ctx'), may hold values from -6 to 6
- cotangent: float32 [1024, 16384], P('ch', 'ctx'), may hold values from -6 to 6
Outputs:
- output: float32 [1024, 16384], P('ch', 'ctx')
- grad_inputs: float32 [3, 1024, 16384], P(None, 'ch', 'ctx')
- grad_filters: float32 [64, 16384], P('ch', 'ctx')
All inputs are finite; a program needn't handle non-finite values.
Results may differ from a plain program's by a relative error of at most 0.00045.
Values may be sent and summed in bfloat16 or wider, within the bound.
No kernel may reach another device: no remote copies, remote signals or barrier semaphores. Data moves between devices by JAX's collectives and lax.ppermute only.
A program may use at most 64 MiB of HBM per device.

v0:
```python
import functools
import math

import jax
import jax.numpy as jnp
import ml_dtypes
import numpy as np
from jax import lax
from jax.experimental import pallas as pl
from jax.experimental.pallas import tpu as pltpu
from jax.sharding import PartitionSpec as P

BF16 = jnp.bfloat16
F32 = jnp.float32
LANES = 128
ROWS = 24
IN_COT, IN_COT_REST, IN_FILT, IN_FILT_REST = 12, 16, 20, 22
OUT_LONG, OUT_GRAD, OUT_FILT, OUT_RIM, OUT_REST = 0, 4, 8, 10, 12


def halves(array):
    array = np.asarray(array, np.float32)
    high = array.astype(ml_dtypes.bfloat16)
    low = (array - high.astype(np.float32)).astype(ml_dtypes.bfloat16)
    return high, low


@functools.lru_cache(maxsize=None)
def tables(pieces, length, scale):
    blocks = 2 * pieces
    total = blocks * length
    freq = np.arange(blocks)[:, None]
    angle = 2.0 * np.pi * ((freq * np.arange(pieces)[None, :]) % blocks) / blocks
    cos, sin = np.cos(angle), np.sin(angle)
    outer = np.block([[cos, sin], [-sin, cos]])
    back = np.block([[cos.T, sin.T], [sin.T, -cos.T]]) * (scale / total)
    angle = 2.0 * np.pi * ((freq * np.arange(length)[None, :]) % total) / total
    twiddle = np.stack([np.cos(angle), -np.sin(angle)]).astype(np.float32)
    count = np.arange(length)
    angle = 2.0 * np.pi * ((count[:, None] * count[None, :]) % length) / length
    cos, sin = np.cos(angle), np.sin(angle)
    inner = np.block([[cos, -sin], [sin, cos]])
    return (*halves(outer), *halves(back), twiddle, *halves(inner))


def split(value):
    high = value.astype(BF16)
    return high, (value - high.astype(F32)).astype(BF16)


def product3(left, right):
    def dot(a, b):
        return jnp.dot(a, b, preferred_element_type=F32)

    return dot(left[0], right[0]) + (dot(left[1], right[0]) + dot(left[0], right[1]))


def put(scratch, row, value):
    scratch[pl.ds(row, value.shape[0], stride=ROWS), :] = value


def put_block(scratch, row, value):
    for half in range(value.shape[1] // LANES):
        put(scratch, row + half, value[:, half * LANES : (half + 1) * LANES])


def put_split(scratch, row, rest, value):
    high = value.astype(BF16).astype(F32)
    put_block(scratch, row, high)
    put_block(scratch, rest, value - high)


def pack_kernel(x_ref, cot_ref, filt_ref, out_ref, scratch):
    pieces = filt_ref.shape[0]
    for stream in range(3):
        for side in range(2):
            block = x_ref[stream, side * pieces : (side + 1) * pieces, :].astype(F32)
            put_block(scratch, (stream * 2 + side) * 2, block)
    for side in range(2):
        block = cot_ref[side * pieces : (side + 1) * pieces, :]
        put_split(scratch, IN_COT + 2 * side, IN_COT_REST + 2 * side, block)
    put_split(scratch, IN_FILT, IN_FILT_REST, filt_ref[...])
    out_ref[...] = scratch[...].astype(BF16)


def conv_kernel(
    r_ref,
    w_ref,
    outer_hi,
    outer_lo,
    back_hi,
    back_lo,
    twiddle,
    inner_hi,
    inner_lo,
    out_ref,
    scratch,
):
    pieces = r_ref.shape[0] // ROWS
    taps = 7
    scratch[...] = r_ref[...].astype(F32)

    def row(index):
        return scratch[pl.ds(index, pieces, stride=ROWS), :]

    def block(index):
        return jnp.concatenate([row(index), row(index + 1)], axis=1)

    row_number = lax.broadcasted_iota(jnp.int32, (pieces, LANES), 0)
    lane_number = lax.broadcasted_iota(jnp.int32, (pieces, LANES), 1)
    rim = jnp.zeros((pieces, LANES), F32)
    featured = []
    for stream in range(3):
        for side in range(2):
            place = stream * 2 + side
            signal = block(place * 2)
            before = jnp.where(row_number == 0, 0.0, pltpu.roll(signal[:, LANES:], 1, 0))
            moved = pltpu.roll(before, (16 * place + 6) % LANES, 1)
            inside = (lane_number >= 16 * place) & (lane_number < 16 * place + taps - 1)
            rim = jnp.where(inside, moved, rim)
            extended = jnp.concatenate([before, signal], axis=1)
            total = w_ref[place * taps] * signal
            for offset in range(1, taps):
                shifted = pltpu.roll(extended, offset, 1)[:, LANES:]
                total = total + w_ref[place * taps + offset] * shifted
            featured.append(total)
    query, key, value = featured[0:2], featured[2:4], featured[4:6]
    cot = [block(IN_COT + 2 * side) + block(IN_COT_REST + 2 * side) for side in range(2)]
    prod = [key[side] * value[side] for side in range(2)]
    mixed = [cot[side] * query[side] for side in range(2)]
    filt = block(IN_FILT) + block(IN_FILT_REST)
    length = filt.shape[1]

    outer = (outer_hi[...], outer_lo[...])
    inner = (inner_hi[...], inner_lo[...])
    back = (back_hi[...], back_lo[...])
    turn_re, turn_im = twiddle[0], twiddle[1]
    count = 2 * pieces

    signals = jnp.concatenate(
        [jnp.concatenate(prod, axis=0), jnp.concatenate(mixed, axis=0)], axis=1
    )
    spread = product3(outer, split(signals))
    spread_f = product3((outer[0][:, :pieces], outer[1][:, :pieces]), split(filt))

    def turned(re, im):
        return jnp.concatenate([re * turn_re - im * turn_im, re * turn_im + im * turn_re], axis=1)

    parts = [spread[:, :length], spread[:, length:], spread_f]
    stacked = jnp.concatenate([turned(part[:count], part[count:]) for part in parts], axis=0)
    spectra = product3(split(stacked), inner)
    z_re, z_im = spectra[:count, :length], spectra[:count, length:]
    m_re, m_im = spectra[count : 2 * count, :length], spectra[count : 2 * count, length:]
    f_re, f_im = spectra[2 * count :, :length], spectra[2 * count :, length:]
    long_re, long_im = z_re * f_re - z_im * f_im, -(z_re * f_im + z_im * f_re)
    grad_re, grad_im = m_re * f_re + m_im * f_im, m_re * f_im - m_im * f_re
    tail_re, tail_im = z_re * m_re + z_im * m_im, z_im * m_re - z_re * m_im
    stacked = jnp.concatenate(
        [
            jnp.concatenate([long_re, long_im], axis=1),
            jnp.concatenate([grad_re, grad_im], axis=1),
            jnp.concatenate([tail_re, tail_im], axis=1),
        ],
        axis=0,
    )
    inside = product3(split(stacked), inner)

    def upright(start):
        re, im = inside[start : start + count, :length], inside[start : start + count, length:]
        return jnp.concatenate([re * turn_re - im * turn_im, re * turn_im + im * turn_re], axis=0)

    columns = jnp.concatenate([upright(0), upright(count), upright(2 * count)], axis=1)
    restored = product3(back, split(columns))

    put_split(scratch, OUT_FILT, OUT_FILT + OUT_REST, restored[:pieces, 2 * length :])
    for side in range(2):
        rows = slice(side * pieces, (side + 1) * pieces)
        long_out = restored[rows, :length]
        grad_long = restored[rows, length : 2 * length]
        put_split(scratch, OUT_LONG + 2 * side, OUT_LONG + OUT_REST + 2 * side, long_out)
        put_split(scratch, OUT_GRAD + 2 * side, OUT_GRAD + OUT_REST + 2 * side, grad_long)
        skip = w_ref[6 * taps + side]
        first = slice(0, LANES)
        grad_query = cot[side][:, first] * (long_out[:, first] + skip * prod[side][:, first])
        grad_product = grad_long[:, first] + skip * mixed[side][:, first]
        grads = (
            grad_query,
            grad_product * value[side][:, first],
            grad_product * key[side][:, first],
        )
        for stream in range(3):
            place = stream * 2 + side
            after = pltpu.roll(grads[stream], pieces - 1, 0)
            after = jnp.where(row_number == pieces - 1, 0.0, after)
            moved = pltpu.roll(after, 16 * place + 8, 1)
            inside_rim = (lane_number >= 16 * place + 8) & (lane_number < 16 * place + 8 + taps - 1)
            rim = jnp.where(inside_rim, moved, rim)
    high = rim.astype(BF16).astype(F32)
    put(scratch, OUT_RIM, high)
    put(scratch, OUT_RIM + OUT_REST, rim - high)
    put(scratch, OUT_RIM + 1, jnp.zeros_like(rim))
    put(scratch, OUT_RIM + 1 + OUT_REST, jnp.zeros_like(rim))
    out_ref[...] = scratch[...].astype(BF16)


def local_kernel(r_ref, x_ref, w_ref, skip_ref, cot_ref, out_ref, grad_ref, scratch):
    pieces = r_ref.shape[0] // ROWS
    taps = w_ref.shape[2]
    length = x_ref.shape[2]
    scratch[...] = r_ref[...].astype(F32)

    def row(index):
        first = scratch[pl.ds(index, pieces, stride=ROWS), :]
        return first + scratch[pl.ds(index + OUT_REST, pieces, stride=ROWS), :]

    def block(index):
        return jnp.concatenate([row(index), row(index + 1)], axis=1)

    rim = row(OUT_RIM)
    for side in range(2):
        rows = slice(side * pieces, (side + 1) * pieces)
        weights = [w_ref[stream, rows, :] for stream in range(3)]
        featured = []
        for stream in range(3):
            place = stream * 2 + side
            signal = x_ref[stream, rows, :].astype(F32)
            before = pltpu.roll(rim, LANES - taps + 1 - 16 * place, 1)
            extended = jnp.concatenate([before, signal], axis=1)
            total = weights[stream][:, 0:1] * signal
            for offset in range(1, taps):
                shifted = pltpu.roll(extended, offset, 1)[:, LANES:]
                total = total + weights[stream][:, offset : offset + 1] * shifted
            featured.append(total)
        query, key, value = featured
        cot = cot_ref[rows, :]
        skip = skip_ref[rows, :]
        prod = key * value
        mixer = block(OUT_LONG + 2 * side) + skip * prod
        out_ref[rows, :] = query * mixer
        grad_product = block(OUT_GRAD + 2 * side) + skip * (cot * query)
        grads = (cot * mixer, grad_product * value, grad_product * key)
        for stream in range(3):
            place = stream * 2 + side
            after = pltpu.roll(rim, LANES - 16 * place - 8, 1)
            extended = jnp.concatenate([grads[stream], after], axis=1)
            total = weights[stream][:, 0:1] * grads[stream]
            for offset in range(1, taps):
                shifted = pltpu.roll(extended, length + LANES - offset, 1)[:, :length]
                total = total + weights[stream][:, offset : offset + 1] * shifted
            grad_ref[stream, rows, :] = total


def call(kernel, out_shape, operands, scratch, smem=(), flops=0):
    specs = [
        pl.BlockSpec(memory_space=pltpu.SMEM if place in smem else pltpu.VMEM)
        for place in range(len(operands))
    ]
    outs = jax.tree.map(lambda _: pl.BlockSpec(memory_space=pltpu.VMEM), out_shape)
    return pl.pallas_call(
        kernel,
        out_shape=out_shape,
        in_specs=specs,
        out_specs=outs,
        scratch_shapes=scratch,
        compiler_params=pltpu.CompilerParams(vmem_limit_bytes=24 * 1024 * 1024),
        cost_estimate=pl.CostEstimate(flops=flops, bytes_accessed=1 << 21, transcendentals=0),
    )(*operands)


def shards(inputs, short_weight, skip, filters, cotangent):
    pieces = lax.axis_size("ctx")
    owners = lax.axis_size("ch")
    position = lax.axis_index("ctx")
    _, channels, length = inputs.shape
    taps = short_weight.shape[2]
    owned = filters.shape[0]
    scale = 1.0 / math.sqrt(pieces * length)
    packed = jax.ShapeDtypeStruct((pieces * ROWS, LANES), BF16)
    room = [pltpu.VMEM((pieces * ROWS, LANES), F32)]

    def transposed(array):
        array = lax.all_to_all(array.reshape(pieces, ROWS, LANES), "ctx", 0, 0)
        return array.reshape(pieces * ROWS, LANES)

    copies = jnp.broadcast_to(filters[None], (owners, owned, length))
    every = lax.all_to_all(copies, "ch", 0, 0).reshape(pieces, length)
    sent = call(pack_kernel, packed, (inputs, cotangent, every), room)
    received = transposed(sent)

    own = lax.dynamic_slice_in_dim(short_weight.reshape(3, 2, pieces, taps), position, 1, 2)
    own_skip = lax.dynamic_slice_in_dim(skip.reshape(2, pieces), position, 1, 1)
    scalars = jnp.concatenate([own.reshape(-1), own_skip.reshape(-1)])
    constants = [jnp.asarray(table) for table in tables(pieces, length, scale)]
    sent = call(
        conv_kernel, packed, (received, scalars, *constants), room, smem=(1,), flops=1500000000
    )
    received = transposed(sent)

    lines = received.reshape(pieces, ROWS, LANES)
    rounded = lines[:, OUT_FILT : OUT_FILT + 2].astype(F32)
    rest = lines[:, OUT_FILT + OUT_REST : OUT_FILT + OUT_REST + 2].astype(F32)
    partial = (rounded + rest).reshape(owners, owned, length)
    terms = lax.all_to_all(partial, "ch", 0, 0)
    output, grad_inputs = call(
        local_kernel,
        (
            jax.ShapeDtypeStruct((channels, length), F32),
            jax.ShapeDtypeStruct((3, channels, length), F32),
        ),
        (received, inputs, short_weight, skip[:, None], cotangent),
        room,
    )
    grad_filters = terms.sum(axis=0)
    return (output, grad_inputs, grad_filters)


def solution(mesh):
    in_specs = (P(None, "ch", "ctx"), P(None, "ch", None), P("ch"), P("ch", "ctx"), P("ch", "ctx"))
    out_specs = (P("ch", "ctx"), P(None, "ch", "ctx"), P("ch", "ctx"))
    return jax.shard_map(shards, mesh=mesh, in_specs=in_specs, out_specs=out_specs, check_vma=False)
```

profile of v0, /device:TPU:1, one launch (start us, length us, event | category | flops | bytes accessed | tf_op | source)
XLA Modules:
  0.0 82.6 jit_solution(2656668167476756717)
XLA Ops:
  0.6 0.0 copy-start
  0.6 0.7 broadcast_in_dim.4
  1.4 14.1 %all_to_all.20 = f32[8,8,256]{2,1,0:T(8,128)S(1)} all-to-all(f32[8,8,256]{2,1,0:T(8,128)S(1)} %broadcast_in_dim.4), channel_id=1, replica_groups=mesh['ctx'=64,'ch'=8] {'ch'}, dimensions={0} | all-to-all | bytes 131072 | tf_op jit(solution)/shard_map/all_to_all | solution.py:286
  15.5 0.0 copy-done
  15.5 0.0 copy-start.1
  15.5 0.9 %copy-done.1 = f32[128,256]{1,0:T(8,128)S(1)} copy-done((f32[128,256]{1,0:T(8,128)S(1)}, f32[128,256]{1,0:T(8,128)}, u32[]{:S(2)}) %copy-start.1) | copy-done | bytes 131096
  16.4 0.0 copy-start.4
  16.4 0.0 copy-start.7
  16.4 0.0 copy-start.8
  16.4 0.0 copy-start.9
  16.4 0.9 %shard_map.139 = bf16[1536,128]{1,0:T(8,128)(2,1)} custom-call(bf16[3,128,256]{2,1,0:T(8,128)(2,1)S(1)} %copy-done, f32[128,256]{1,0:T(8,128)S(1)} %copy-done.1, f32[64,256]{1,0:T(8,128)S(1)} %bitcast.13), custom_call_target="tpu_custom_call" | custom-call | bytes 2097152 | tf_op jit(solution)/shard_map/pallas_call | solution.py:259
  17.3 0.0 copy-start.3
  17.3 0.0 copy-start.10
  17.3 0.0 copy-start.5
  17.3 12.8 %all-to-all-start.1 = ((bf16[64,24,128]{2,1,0:T(8,128)(2,1)}), bf16[64,24,128]{2,1,0:T(8,128)(2,1)S(1)}, u32[]{:S(2)}, u32[]{:S(2)}) async-start(bf16[64,24,128]{2,1,0:T(8,128)(2,1)} %bitcast.1), calls=%async_computation.1 | async-start | bytes 786432 | tf_op jit(solution)/shard_map/all_to_all | solution.py:282
  30.1 0.0 copy-start.6
  30.1 0.0 copy-done.10
  30.1 0.1 reshape.40
  30.2 0.1 constant_dynamic-slice_fusion
  30.3 0.1 copy.21
  30.4 0.0 copy-start.11
  30.4 0.1 reshape.41
  30.5 0.6 copy-done.11
  31.1 0.1 reshape.42
  31.2 0.2 dynamic-slice_reduce_fusion
  31.4 0.1 pad_maximum_fusion.w_ref
  31.4 13.1 %all-to-all-done.1 = bf16[64,24,128]{2,1,0:T(8,128)(2,1)S(1)} async-done(((bf16[64,24,128]{2,1,0:T(8,128)(2,1)}), bf16[64,24,128]{2,1,0:T(8,128)(2,1)S(1)}, u32[]{:S(2)}, u32[]{:S(2)}) %all-to-all-start.1) | async-done | bytes 393248 | tf_op jit(solution)/shard_map/all_to_all | solution.py:282
  44.6 0.0 copy-done.4
  44.6 0.0 copy-done.7
  44.6 0.0 copy-done.8
  44.6 0.0 copy-done.9
  44.6 0.0 copy-done.3
  44.6 0.0 copy-done.5
  44.6 0.0 copy-done.6
  44.6 4.0 %shard_map.140 = bf16[1536,128]{1,0:T(8,128)(2,1)S(1)} custom-call(bf16[1536,128]{1,0:T(8,128)(2,1)S(1)} %bitcast.11, f32[44]{0:T(128)S(1)} %pad_maximum_fusion.w_ref, bf16[256,128]{1,0:T(8,128)(2,1)S(1)} %copy-done.6, bf16[256,128]{1,0:T(8,128)(2,1)S(1)} %copy-done.7, bf16[128,256]{1,0:T(8,128)(2,1)S(1)} %copy-done.8, bf16[128,256]{1,0:T(8,128)(2,1)S(1)} %copy-done.9, ...), custom_call_target="tpu_custom_call" | custom-call | flops 1500000000 | bytes 2097152 | tf_op jit(solution)/shard_map/pallas_call | solution.py:259
  48.6 20.2 %all_to_all.21 = bf16[64,24,128]{2,1,0:T(8,128)(2,1)S(1)} all-to-all(bf16[64,24,128]{2,1,0:T(8,128)(2,1)S(1)} %bitcast.12), channel_id=1, replica_groups=mesh['ctx'=64,'ch'=8] {'ctx'}, dimensions={0} | all-to-all | bytes 786432 | tf_op jit(solution)/shard_map/all_to_all | solution.py:282
  68.9 0.7 reshape.46
  69.6 7.5 %all-to-all-start.3 = ((f32[8,8,256]{2,1,0:T(8,128)}), f32[8,8,256]{2,1,0:T(8,128)S(1)}, u32[]{:S(2)}, u32[]{:S(2)}) async-start(f32[8,8,256]{2,1,0:T(8,128)} %reshape.46), calls=%async_computation.3 | async-start | bytes 131072 | tf_op jit(solution)/shard_map/all_to_all | solution.py:303
  77.1 0.0 copy-start.2
  77.1 0.1 copy.19.w_ref
  77.3 0.1 copy.20.skip_ref
  77.4 0.6 copy-done.2
  78.0 3.7 %shard_map.141 = (f32[128,256]{1,0:T(8,128)}, f32[3,128,256]{2,1,0:T(8,128)}) custom-call(bf16[1536,128]{1,0:T(8,128)(2,1)S(1)} %bitcast.10, bf16[3,128,256]{2,1,0:T(8,128)(2,1)S(1)} %copy-done, f32[3,128,7]{2,1,0:T(8,128)S(1)} %copy.19.w_ref, f32[128,1]{1,0:T(8,128)S(1)} %copy.20.skip_ref, f32[128,256]{1,0:T(8,128)S(1)} %copy-done.2), custom_call_target="tpu_custom_call" | custom-call | bytes 2097152 | tf_op jit(solution)/shard_map/pallas_call | solution.py:259
  81.7 0.3 all-to-all-done.3
  82.0 0.6 reduce_sum.9
  (1 shorter events, 0.0 us)
Async XLA Ops:
  0.6 14.8 %copy-start = (bf16[3,128,256]{2,1,0:T(8,128)(2,1)S(1)}, bf16[3,128,256]{2,1,0:T(8,128)(2,1)}, u32[]{:S(2)}) copy-start(bf16[3,128,256]{2,1,0:T(8,128)(2,1)} %x_ref.3) | copy-start | bytes 589828
  15.5 0.9 %copy-start.1 = (f32[128,256]{1,0:T(8,128)S(1)}, f32[128,256]{1,0:T(8,128)}, u32[]{:S(2)}) copy-start(f32[128,256]{1,0:T(8,128)} %cot_ref.3) | copy-start | bytes 393220
  16.4 28.2 %copy-start.4 = (bf16[512,512]{1,0:T(8,128)(2,1)S(1)}, bf16[512,512]{1,0:T(8,128)(2,1)}, u32[]{:S(2)}) copy-start(bf16[512,512]{1,0:T(8,128)(2,1)} %constant.32.clone.inner_lo) | copy-start | bytes 1572868
  16.4 28.2 %copy-start.7 = (bf16[256,128]{1,0:T(8,128)(2,1)S(1)}, bf16[256,128]{1,0:T(8,128)(2,1)}, u32[]{:S(2)}) copy-start(bf16[256,128]{1,0:T(8,128)(2,1)} %constant.27.clone.outer_lo) | copy-start | bytes 196612
  16.4 28.2 %copy-start.8 = (bf16[128,256]{1,0:T(8,128)(2,1)S(1)}, bf16[128,256]{1,0:T(8,128)(2,1)}, u32[]{:S(2)}) copy-start(bf16[128,256]{1,0:T(8,128)(2,1)} %constant.28.clone.back_hi) | copy-start | bytes 196612
  16.4 28.2 %copy-start.9 = (bf16[128,256]{1,0:T(8,128)(2,1)S(1)}, bf16[128,256]{1,0:T(8,128)(2,1)}, u32[]{:S(2)}) copy-start(bf16[128,256]{1,0:T(8,128)(2,1)} %constant.29.clone.back_lo) | copy-start | bytes 196612
  17.3 27.3 %copy-start.3 = (bf16[512,512]{1,0:T(8,128)(2,1)S(1)}, bf16[512,512]{1,0:T(8,128)(2,1)}, u32[]{:S(2)}) copy-start(bf16[512,512]{1,0:T(8,128)(2,1)} %constant.31.clone.inner_hi) | copy-start | bytes 1572868
  17.3 12.8 %copy-start.10 = (f32[3,128,7]{1,2,0:T(8,128)S(1)}, f32[3,128,7]{1,2,0:T(8,128)}, u32[]{:S(2)}) copy-start(f32[3,128,7]{1,2,0:T(8,128)} %param.13) | copy-start | bytes 32260
  17.3 27.3 %copy-start.5 = (f32[2,128,256]{2,1,0:T(8,128)S(1)}, f32[2,128,256]{2,1,0:T(8,128)}, u32[]{:S(2)}) copy-start(f32[2,128,256]{2,1,0:T(8,128)} %constant.30.clone.twiddle) | copy-start | bytes 786436
  17.3 27.2 %all-to-all-start.1 = ((bf16[64,24,128]{2,1,0:T(8,128)(2,1)}), bf16[64,24,128]{2,1,0:T(8,128)(2,1)S(1)}, u32[]{:S(2)}, u32[]{:S(2)}) async-start(bf16[64,24,128]{2,1,0:T(8,128)(2,1)} %bitcast.1), calls=%async_computation.1 | async-start | bytes 786432 | tf_op jit(solution)/shard_map/all_to_all | solution.py:282
  30.1 14.5 %copy-start.6 = (bf16[256,128]{1,0:T(8,128)(2,1)S(1)}, bf16[256,128]{1,0:T(8,128)(2,1)}, u32[]{:S(2)}) copy-start(bf16[256,128]{1,0:T(8,128)(2,1)} %constant.26.clone.outer_hi) | copy-start | bytes 196612
  30.4 0.7 copy-start.11
  69.6 12.4 %all-to-all-start.3 = ((f32[8,8,256]{2,1,0:T(8,128)}), f32[8,8,256]{2,1,0:T(8,128)S(1)}, u32[]{:S(2)}, u32[]{:S(2)}) async-start(f32[8,8,256]{2,1,0:T(8,128)} %reshape.46), calls=%async_computation.3 | async-start | bytes 131072 | tf_op jit(solution)/shard_map/all_to_all | solution.py:303
  77.1 0.9 %copy-start.2 = (f32[128,256]{1,0:T(8,128)S(1)}, f32[128,256]{1,0:T(8,128)}, u32[]{:S(2)}) copy-start(f32[128,256]{1,0:T(8,128)} %cot_ref.3) | copy-start | bytes 393220
where the time goes:
time: 83 us; the launch traced here: 82.6 us
  blocking collectives  34.3 us (41%)
  starting transfers between devices  20.3 us (24%)
  waiting for transfers between devices  13.4 us (16%)
  Pallas kernels  8.65 us (10%)
  local copies, waits for them, and re-layouts  4.47 us (5%)
    all_to_all x1, blocking collectives, transposed(): array = lax.all_to_all(array.reshape(pieces, ROWS, LANES), 'ctx', 0, 0)  20.2 us
    all_to_all x1, blocking collectives, shards(): every = lax.all_to_all(copies, 'ch', 0, 0).reshape(pieces, length)  14.1 us
    all_to_all x1, waiting for transfers between devices, transposed(): array = lax.all_to_all(array.reshape(pieces, ROWS, LANES), 'ctx', 0, 0)  13.1 us
    all_to_all x1, starting transfers between devices, transposed(): array = lax.all_to_all(array.reshape(pieces, ROWS, LANES), 'ctx', 0, 0)  12.8 us
    pallas_call x3, Pallas kernels, call(): pl.pallas_call(kernel, out_shape=out_shape, in_specs=specs, out_specs=out...  8.65 us
    all_to_all x1, starting transfers between devices, shards(): terms = lax.all_to_all(partial, 'ch', 0, 0)  7.53 us
    unnamed x26, local copies, waits for them, and re-layouts  2.43 us
  transfers between devices with their start and end apart: 2, of which 2 were waited for; matrix products, arithmetic and copies ran while one was open for 1% of the time, Pallas kernels for 4%

commit v1 on v0

v1 whole, which is shorter than its diff:
```python
import functools
import math

import jax
import jax.numpy as jnp
import ml_dtypes
import numpy as np
from jax import lax
from jax.experimental import pallas as pl
from jax.experimental.pallas import tpu as pltpu
from jax.sharding import PartitionSpec as P

BF16 = jnp.bfloat16
F32 = jnp.float32
LANES = 128
TAPS = 7
IN_COT, IN_FILT, IN_TOPS, IN_ROWS = 12, 16, 18, 20
CROSS_FILT, CROSS_GRAD, CROSS_TOPS, CROSS_ROWS = 0, 2, 4, 5
OUT_LONG, OUT_GRAD, OUT_FILT, OUT_RIM, OUT_HEAD, OUT_ROWS = 0, 4, 8, 10, 11, 12
RIM = TAPS - 1
TOP_LANE = 12 * RIM
REACH = 125.0


def halves(array):
    array = np.asarray(array, np.float32)
    high = array.astype(ml_dtypes.bfloat16)
    low = (array - high.astype(np.float32)).astype(ml_dtypes.bfloat16)
    return high, low


@functools.lru_cache(maxsize=None)
def tables(pieces, length, scale):
    blocks = 2 * pieces
    total = blocks * length
    freq = np.arange(blocks)[:, None]
    angle = 2.0 * np.pi * ((freq * np.arange(pieces)[None, :]) % blocks) / blocks
    cos, sin = np.cos(angle), np.sin(angle)
    outer = np.block([[cos, sin], [-sin, cos]])
    back = np.block([[cos.T, sin.T], [sin.T, -cos.T]]) * (scale / total)
    angle = 2.0 * np.pi * ((freq * np.arange(length)[None, :]) % total) / total
    twiddle = np.stack([np.cos(angle), -np.sin(angle)]).astype(np.float32)
    count = np.arange(length)
    angle = 2.0 * np.pi * ((count[:, None] * count[None, :]) % length) / length
    cos, sin = np.cos(angle), np.sin(angle)
    inner = np.block([[cos, -sin], [sin, cos]])
    return (*halves(outer), *halves(back), twiddle, *halves(inner))


def split(value):
    high = value.astype(BF16)
    return high, (value - high.astype(F32)).astype(BF16)


def product3(left, right):
    def dot(a, b):
        return jnp.dot(a, b, preferred_element_type=F32)

    return dot(left[0], right[0]) + (dot(left[1], right[0]) + dot(left[0], right[1]))


def encoded(value):
    top = jnp.max(jnp.abs(value), axis=1, keepdims=True)
    top = (jnp.maximum(top, 1e-30) * 1.008).astype(BF16).astype(F32)
    size = jnp.sqrt(jnp.abs(value) * (1.0 / top))
    code = jnp.exp2(size * (2.0 * REACH) - REACH)
    return jnp.where(value < 0.0, -code, code), top


def decoded(code, top):
    size = (jnp.log2(jnp.abs(code)) + REACH) * (0.5 / REACH)
    value = size * size * top
    return jnp.where(code < 0.0, -value, value)


class Lines:
    def __init__(self, ref, rows):
        self.ref, self.rows = ref, rows
        self.count = ref.shape[0] // rows

    def get(self, row):
        return self.ref[pl.ds(row, self.count, stride=self.rows), :]

    def put(self, row, value):
        self.ref[pl.ds(row, self.count, stride=self.rows), :] = value

    def get_block(self, row):
        return jnp.concatenate([self.get(row), self.get(row + 1)], axis=1)

    def put_block(self, row, value):
        self.put(row, value[:, :LANES])
        self.put(row + 1, value[:, LANES:])


def in_lanes(columns, first, like):
    lane = lax.broadcasted_iota(jnp.int32, like.shape, 1)
    for place, column in enumerate(columns):
        like = jnp.where(lane == first + place, column, like)
    return like


def exchanged(value, member, owners):
    size = value.shape[0] // owners
    step = 1
    while step < owners:
        order = [place ^ step for place in range(owners)]
        swapped = jnp.concatenate([value[k * size : (k + 1) * size] for k in order], axis=0)
        value = jnp.where((member & step) != 0, swapped, value)
        step *= 2
    return value


def pack_kernel(
    owners, member_ref, x_hbm, cot_hbm, filt_hbm, out_ref, scratch, x_ref, cot_ref, filt_ref, sems
):
    copies = [pltpu.make_async_copy(x_hbm.at[place], x_ref.at[place], sems.at[place]) for place in range(3)]
    copies.append(pltpu.make_async_copy(cot_hbm, cot_ref, sems.at[3]))
    copies.append(pltpu.make_async_copy(filt_hbm, filt_ref, sems.at[4]))
    for copy in copies:
        copy.start()
    lines = Lines(scratch, IN_ROWS)
    pieces = lines.count
    member = member_ref[0]
    for stream in range(3):
        copies[stream].wait()
        for side in range(2):
            rows = slice(side * pieces, (side + 1) * pieces)
            block = x_ref[stream, rows, :].astype(F32)
            lines.put_block((stream * 2 + side) * 2, exchanged(block, member, owners))
    tops = []
    copies[3].wait()
    for side in range(2):
        block = exchanged(cot_ref[side * pieces : (side + 1) * pieces, :], member, owners)
        code, top = encoded(block)
        tops.append(top)
        lines.put_block(IN_COT + 2 * side, code)
    copies[4].wait()
    code, top = encoded(filt_ref[...])
    lines.put_block(IN_FILT, jnp.concatenate([code] * owners, axis=0))
    tops.append(jnp.concatenate([top] * owners, axis=0))
    blank = jnp.zeros((pieces, LANES), F32)
    lines.put(IN_TOPS, in_lanes(tops, 0, blank))
    lines.put(IN_TOPS + 1, blank)
    out_ref[...] = scratch[...].astype(BF16)


def turned(re, im, twiddle):
    turn_re, turn_im = twiddle[0], twiddle[1]
    return re * turn_re - im * turn_im, re * turn_im + im * turn_re


def upright(spectra, inner, twiddle, count):
    length = spectra.shape[1] // 2
    inside = product3(split(spectra), inner)
    columns = []
    for start in range(0, spectra.shape[0], count):
        rows = slice(start, start + count)
        pair = turned(inside[rows, :length], inside[rows, length:], twiddle)
        columns.append(jnp.concatenate(pair, axis=0))
    return jnp.concatenate(columns, axis=1)


def rim_lanes(value, place, rim):
    lane = lax.broadcasted_iota(jnp.int32, rim.shape, 1)
    high = value.astype(BF16).astype(F32)
    both = jnp.where(lane < RIM, high, pltpu.roll(value - high, RIM, 1))
    start = 2 * RIM * place
    moved = pltpu.roll(both, start, 1) if start else both
    return jnp.where((lane >= start) & (lane < start + 2 * RIM), moved, rim)


def forward_kernel(
    r_ref,
    w_ref,
    outer_hi,
    outer_lo,
    back_hi,
    back_lo,
    twiddle,
    inner_hi,
    inner_lo,
    cross_ref,
    spec_ref,
    kept_ref,
    scratch,
    cross_scratch,
):
    scratch[...] = r_ref[...].astype(F32)
    lines = Lines(scratch, IN_ROWS)
    cross = Lines(cross_scratch, CROSS_ROWS)
    pieces = lines.count
    count = 2 * pieces
    length = 2 * LANES
    tops = lines.get(IN_TOPS)
    row_number = lax.broadcasted_iota(jnp.int32, (pieces, LANES), 0)
    head = jnp.zeros((pieces, LANES), F32)
    featured = []
    for stream in range(3):
        for side in range(2):
            place = stream * 2 + side
            signal = lines.get_block(place * 2)
            before = jnp.where(row_number == 0, 0.0, pltpu.roll(signal[:, LANES:], 1, 0))
            extended = jnp.concatenate([before, signal], axis=1)
            total = w_ref[place * TAPS] * signal
            for offset in range(1, TAPS):
                shifted = pltpu.roll(extended, offset, 1)[:, LANES:]
                total = total + w_ref[place * TAPS + offset] * shifted
            featured.append(total)
            head = rim_lanes(total[:, :LANES], place, head)
    query, key, value = featured[0:2], featured[2:4], featured[4:6]
    cot = [
        decoded(lines.get_block(IN_COT + 2 * side), tops[:, side : side + 1]) for side in range(2)
    ]
    prod = [key[side] * value[side] for side in range(2)]
    mixed = [cot[side] * query[side] for side in range(2)]
    for side in range(2):
        for place, array in enumerate((prod, mixed, key, value, cot)):
            kept_ref[side * 5 + place] = array[side][:, :LANES]
    kept_ref[10] = head

    signals = jnp.concatenate(
        [jnp.concatenate(prod, axis=0), jnp.concatenate(mixed, axis=0)], axis=1
    )
    spread = product3((outer_hi[...], outer_lo[...]), split(signals))
    parts = []
    for start in (0, length):
        part = spread[:, start : start + length]
        parts.append(jnp.concatenate(turned(part[:count], part[count:], twiddle), axis=1))
    inner = (inner_hi[...], inner_lo[...])
    spectra = product3(split(jnp.concatenate(parts, axis=0)), inner)
    spec_ref[...] = spectra
    z_re, z_im = spectra[:count, :length], spectra[:count, length:]
    m_re, m_im = spectra[count:, :length], spectra[count:, length:]
    tail = jnp.concatenate([z_re * m_re + z_im * m_im, z_im * m_re - z_re * m_im], axis=1)
    columns = upright(tail, inner, twiddle, count)
    partial = product3((back_hi[:pieces, :], back_lo[:pieces, :]), split(columns))
    code, top = encoded(partial)
    cross.put_block(CROSS_GRAD, code)
    cross.put_block(CROSS_FILT, lines.get_block(IN_FILT))
    blank = jnp.zeros((pieces, LANES), F32)
    cross.put(CROSS_TOPS, in_lanes([tops[:, 2:3], top], 0, blank))
    cross_ref[...] = cross_scratch[...].astype(BF16)


def inverse_kernel(
    cross_ref,
    spec_ref,
    kept_ref,
    w_ref,
    outer_hi,
    outer_lo,
    back_hi,
    back_lo,
    twiddle,
    inner_hi,
    inner_lo,
    out_ref,
    cross_scratch,
    scratch,
):
    cross_scratch[...] = cross_ref[...].astype(F32)
    cross = Lines(cross_scratch, CROSS_ROWS)
    lines = Lines(scratch, OUT_ROWS)
    pieces = lines.count
    count = 2 * pieces
    length = 2 * LANES
    tops = cross.get(CROSS_TOPS)
    filt = decoded(cross.get_block(CROSS_FILT), tops[:, 0:1])
    inner = (inner_hi[...], inner_lo[...])
    spread = product3((outer_hi[:, :pieces], outer_lo[:, :pieces]), split(filt))
    stacked = jnp.concatenate(turned(spread[:count], spread[count:], twiddle), axis=1)
    spectra = product3(split(stacked), inner)
    f_re, f_im = spectra[:, :length], spectra[:, length:]
    z_re, z_im = spec_ref[:count, :length], spec_ref[:count, length:]
    m_re, m_im = spec_ref[count:, :length], spec_ref[count:, length:]
    long_pair = jnp.concatenate(
        [z_re * f_re - z_im * f_im, -(z_re * f_im + z_im * f_re)], axis=1
    )
    grad_pair = jnp.concatenate([m_re * f_re + m_im * f_im, m_re * f_im - m_im * f_re], axis=1)
    columns = upright(jnp.concatenate([long_pair, grad_pair], axis=0), inner, twiddle, count)
    restored = product3((back_hi[...], back_lo[...]), split(columns))
    row_number = lax.broadcasted_iota(jnp.int32, (pieces, LANES), 0)
    rim = jnp.zeros((pieces, LANES), F32)
    long_tops, grad_tops = [], []
    for side in range(2):
        rows = slice(side * pieces, (side + 1) * pieces)
        long_out = restored[rows, :length]
        grad_long = restored[rows, length:]
        code, top = encoded(long_out)
        lines.put_block(OUT_LONG + 2 * side, code)
        long_tops.append(top)
        code, top = encoded(grad_long)
        lines.put_block(OUT_GRAD + 2 * side, code)
        grad_tops.append(top)
        skip = w_ref[6 * TAPS + side]
        prod, mixed, key, value, cot = [kept_ref[side * 5 + place] for place in range(5)]
        grad_product = grad_long[:, :LANES] + skip * mixed
        grad_query = cot * (long_out[:, :LANES] + skip * prod)
        for stream, grad in enumerate((grad_query, grad_product * value, grad_product * key)):
            after = jnp.where(row_number == pieces - 1, 0.0, pltpu.roll(grad, pieces - 1, 0))
            rim = rim_lanes(after, stream * 2 + side, rim)
    lines.put_block(OUT_FILT, cross.get_block(CROSS_GRAD))
    lines.put(OUT_RIM, in_lanes([*long_tops, *grad_tops, tops[:, 1:2]], TOP_LANE, rim))
    lines.put(OUT_HEAD, kept_ref[10])
    out_ref[...] = scratch[...].astype(BF16)


def feature_kernel(x_ref, w_ref, out_ref):
    pieces = x_ref.shape[1] // 2
    for stream in range(3):
        for side in range(2):
            rows = slice(side * pieces, (side + 1) * pieces)
            weights = w_ref[stream, rows, :]
            signal = x_ref[stream, rows, :].astype(F32)
            total = weights[:, 0:1] * signal
            for offset in range(1, TAPS):
                total = total + weights[:, offset : offset + 1] * pltpu.roll(signal, offset, 1)
            out_ref[stream, rows, :] = total


def local_kernel(
    owners,
    r_ref,
    member_ref,
    feat_ref,
    w_ref,
    skip_ref,
    cot_ref,
    out_ref,
    grad_ref,
    tail_ref,
    scratch,
    out_room,
    grad_room,
    tail_room,
    sems,
):
    member = member_ref[0]
    length = cot_ref.shape[1]
    scratch[...] = r_ref[...].astype(F32)
    lines = Lines(scratch, OUT_ROWS)
    pieces = lines.count
    copies = []

    def send(source, target):
        copy = pltpu.make_async_copy(source, target, sems.at[len(copies)])
        copy.start()
        copies.append(copy)

    def block(row, top_place):
        return decoded(lines.get_block(row), tops[:, TOP_LANE + top_place : TOP_LANE + top_place + 1])

    tops = lines.get(OUT_RIM)
    rim = exchanged(tops, member, owners)
    rim = rim + pltpu.roll(rim, LANES - RIM, 1)
    head = exchanged(lines.get(OUT_HEAD), member, owners)
    head = head + pltpu.roll(head, LANES - RIM, 1)
    lane = lax.broadcasted_iota(jnp.int32, (pieces, LANES), 1)

    def first_lanes(array, place):
        start = 2 * RIM * place
        return pltpu.roll(array, LANES - start, 1) if start else array

    for side in range(2):
        rows = slice(side * pieces, (side + 1) * pieces)
        featured = []
        for stream in range(3):
            inside = feat_ref[stream, rows, :]
            left = first_lanes(head, stream * 2 + side)
            left = jnp.where(lane < RIM, left, inside[:, :LANES])
            featured.append(jnp.concatenate([left, inside[:, LANES:]], axis=1))
        query, key, value = featured
        cot = cot_ref[rows, :]
        skip = skip_ref[rows, :]
        long_out = exchanged(block(OUT_LONG + 2 * side, side), member, owners)
        mixer = long_out + skip * (key * value)
        out_room[rows, :] = query * mixer
        send(out_room.at[rows, :], out_ref.at[rows, :])
        grad_long = exchanged(block(OUT_GRAD + 2 * side, 2 + side), member, owners)
        grad_product = grad_long + skip * (cot * query)
        for stream, grad in enumerate((cot * mixer, grad_product * value, grad_product * key)):
            weights = w_ref[stream, rows, :]
            after = first_lanes(rim, stream * 2 + side)
            extended = jnp.concatenate([grad, after], axis=1)
            total = weights[:, 0:1] * grad
            for offset in range(1, TAPS):
                shifted = pltpu.roll(extended, length + LANES - offset, 1)[:, :length]
                total = total + weights[:, offset : offset + 1] * shifted
            grad_room[stream, rows, :] = total
            send(grad_room.at[stream, rows, :], grad_ref.at[stream, rows, :])
    partial = block(OUT_FILT, 4)
    owned = pieces // owners
    total = partial[:owned]
    for place in range(1, owners):
        total = total + partial[place * owned : (place + 1) * owned]
    tail_room[...] = total
    send(tail_room, tail_ref)
    for copy in copies:
        copy.wait()


VMEM_SPEC = pl.BlockSpec(memory_space=pltpu.VMEM)
SMEM_SPEC = pl.BlockSpec(memory_space=pltpu.SMEM)
ANY_SPEC = pl.BlockSpec(memory_space=pl.ANY)


def call(kernel, out_shape, operands, scratch=(), specs=None, flops=0, out_spec=VMEM_SPEC):
    specs = specs or {}
    return pl.pallas_call(
        kernel,
        out_shape=out_shape,
        in_specs=[specs.get(place, VMEM_SPEC) for place in range(len(operands))],
        out_specs=jax.tree.map(lambda _: out_spec, out_shape),
        scratch_shapes=list(scratch),
        compiler_params=pltpu.CompilerParams(vmem_limit_bytes=24 * 1024 * 1024),
        cost_estimate=pl.CostEstimate(flops=flops, bytes_accessed=1 << 20, transcendentals=0),
    )(*operands)


def shards(inputs, short_weight, skip, filters, cotangent):
    pieces = lax.axis_size("ctx")
    owners = lax.axis_size("ch")
    position = lax.axis_index("ctx")
    member = lax.axis_index("ch")
    _, channels, length = inputs.shape
    owned = filters.shape[0]
    count = 2 * pieces
    scale = 1.0 / math.sqrt(pieces * length)
    member_word = member.astype(jnp.int32).reshape(1)

    def shape(*dims, dtype=F32):
        return jax.ShapeDtypeStruct(dims, dtype)

    def room(rows):
        return pltpu.VMEM((pieces * rows, LANES), F32)

    def transposed(array):
        rows = array.shape[0] // pieces
        array = lax.all_to_all(array.reshape(pieces, rows // 2, 2, LANES), "ctx", 0, 0)
        return array.reshape(pieces * rows, LANES)

    sent = call(
        functools.partial(pack_kernel, owners),
        shape(pieces * IN_ROWS, LANES, dtype=BF16),
        (member_word, inputs, cotangent, filters),
        [
            room(IN_ROWS),
            pltpu.VMEM(inputs.shape, BF16),
            pltpu.VMEM(cotangent.shape, F32),
            pltpu.VMEM(filters.shape, F32),
            pltpu.SemaphoreType.DMA((5,)),
        ],
        specs={0: SMEM_SPEC, 1: ANY_SPEC, 2: ANY_SPEC, 3: ANY_SPEC},
    )
    received = transposed(sent)

    group = ((position // owned) ^ member) * owned + position % owned
    own = lax.dynamic_slice_in_dim(short_weight.reshape(3, 2, pieces, TAPS), group, 1, 2)
    own_skip = lax.dynamic_slice_in_dim(skip.reshape(2, pieces), group, 1, 1)
    scalars = jnp.concatenate([own.reshape(-1), own_skip.reshape(-1)])
    constants = [jnp.asarray(table) for table in tables(pieces, length, scale)]
    featured = call(feature_kernel, shape(3, channels, length), (inputs, short_weight))
    skip_column = skip[:, None]
    received, featured, skip_column, short_rows = lax.optimization_barrier(
        (received, featured, skip_column, short_weight)
    )

    cross, spectra, kept = call(
        forward_kernel,
        (
            shape(pieces * CROSS_ROWS, LANES, dtype=BF16),
            shape(2 * count, 2 * length),
            shape(11, pieces, LANES),
        ),
        (received, scalars, *constants),
        [room(IN_ROWS), room(CROSS_ROWS)],
        specs={1: SMEM_SPEC},
        flops=800000000,
    )
    partners = [
        (place * owners + shard, place * owners + (shard ^ (place // owned)))
        for place in range(pieces)
        for shard in range(owners)
    ]
    cross = lax.ppermute(cross, ("ctx", "ch"), partners)
    sent = call(
        inverse_kernel,
        shape(pieces * OUT_ROWS, LANES, dtype=BF16),
        (cross, spectra, kept, scalars, *constants),
        [room(CROSS_ROWS), room(OUT_ROWS)],
        specs={3: SMEM_SPEC},
        flops=800000000,
    )
    received = transposed(sent)

    return call(
        functools.partial(local_kernel, owners),
        (shape(channels, length), shape(3, channels, length), shape(owned, length)),
        (received, member_word, featured, short_rows, skip_column, cotangent),
        [
            room(OUT_ROWS),
            pltpu.VMEM((channels, length), F32),
            pltpu.VMEM((3, channels, length), F32),
            pltpu.VMEM((owned, length), F32),
            pltpu.SemaphoreType.DMA((9,)),
        ],
        specs={1: SMEM_SPEC},
        out_spec=ANY_SPEC,
    )


def solution(mesh):
    in_specs = (P(None, "ch", "ctx"), P(None, "ch", None), P("ch"), P("ch", "ctx"), P("ch", "ctx"))
    out_specs = (P("ch", "ctx"), P(None, "ch", "ctx"), P("ch", "ctx"))
    return jax.shard_map(shards, mesh=mesh, in_specs=in_specs, out_specs=out_specs, check_vma=False)
```

time: 83 us -> 72.8 us (0.88)
  blocking collectives: 34.3 us -> 0 us
  starting transfers between devices: 20.3 us -> 32.1 us
  waiting for transfers between devices: 13.4 us -> 23.4 us
  Pallas kernels: 8.65 us -> 11.8 us
    all_to_all x2 -> x0, blocking collectives: 34.3 us -> none  [the longest x1 20.2 us: transposed(): array = lax.all_to_all(array.reshape(pieces, ROWS, LANES), 'ctx', 0, 0)]
    all_to_all x2, starting transfers between devices: 20.3 us -> 31.4 us  [transposed(): lax.all_to_all(array.reshape(pieces, rows // 2, 2, LANES), 'ctx', 0, 0)]
    all_to_all x2, waiting for transfers between devices: 13.4 us -> 23.4 us  [transposed(): lax.all_to_all(array.reshape(pieces, rows // 2, 2, LANES), 'ctx', 0, 0)]
    pallas_call x3 -> x5, Pallas kernels: 8.65 us -> 11.8 us  [call(): pl.pallas_call(kernel, out_shape=out_shape, in_specs=[specs.get(place, VM...]
    broadcast_in_dim x2 -> x0, local copies, waits for them, and re-layouts: 0.85 us -> none  [the longest x1 0.74 us: shards(): copies = jnp.broadcast_to(filters[None], (owners, owned, length))]
    unnamed x26 -> x30, local copies, waits for them, and re-layouts: 2.43 us -> 2.98 us
  transfers between devices with their start and end apart: 2 -> 3, of which waited for: 2 -> 2; matrix products, arithmetic and copies ran while one was open for 1% -> 2% of each run, Pallas kernels for 4% -> 1%
where the time goes in v1:
time: 72.8 us; the launch traced here: 72 us
  starting transfers between devices  32.1 us (44%)
  waiting for transfers between devices  23.4 us (32%)
  Pallas kernels  11.8 us (16%)
  local copies, waits for them, and re-layouts  3.75 us (5%)
  between operations  0.9 us (1%)
    all_to_all x2, starting transfers between devices, transposed(): lax.all_to_all(array.reshape(pieces, rows // 2, 2, LANES), 'ctx', 0, 0)  31.4 us
    all_to_all x2, waiting for transfers between devices, transposed(): lax.all_to_all(array.reshape(pieces, rows // 2, 2, LANES), 'ctx', 0, 0)  23.4 us
    pallas_call x5, Pallas kernels, call(): pl.pallas_call(kernel, out_shape=out_shape, in_specs=[specs.get(place, VM...  11.8 us
    unnamed x30, local copies, waits for them, and re-layouts  2.98 us
  transfers between devices with their start and end apart: 3, of which 2 were waited for; matrix products, arithmetic and copies ran while one was open for 2% of the time, Pallas kernels for 1%

profile of v1, /device:TPU:1, one launch (start us, length us, event | category | flops | bytes accessed | tf_op | source)
XLA Modules:
  0.0 72.0 jit_solution(510422102217837746)
XLA Ops:
  0.6 0.0 copy-start
  0.6 0.9 %copy-done = bf16[3,128,256]{2,1,0:T(8,128)(2,1)S(1)} copy-done((bf16[3,128,256]{2,1,0:T(8,128)(2,1)S(1)}, bf16[3,128,256]{2,1,0:T(8,128)(2,1)}, u32[]{:S(2)}) %copy-start) | copy-done | bytes 196632
  1.6 0.0 copy-start.2
  1.6 0.9 %copy-done.2 = f32[128,256]{1,0:T(8,128)S(1)} copy-done((f32[128,256]{1,0:T(8,128)S(1)}, f32[128,256]{1,0:T(8,128)}, u32[]{:S(2)}) %copy-start.2) | copy-done | bytes 131096
  2.5 0.0 copy-start.4
  2.5 0.7 copy-done.4
  3.2 1.6 %shard_map.139 = bf16[1280,128]{1,0:T(8,128)(2,1)} custom-call(s32[1]{0:T(128)} %bitcast.member_ref, bf16[3,128,256]{2,1,0:T(8,128)(2,1)S(1)} %copy-done, f32[128,256]{1,0:T(8,128)S(1)} %copy-done.2, f32[8,256]{1,0:T(8,128)S(1)} %copy-done.4), custom_call_target="tpu_custom_call" | custom-call | bytes 1048576 | tf_op jit(solution)/shard_map/pallas_call | solution.py:409
  4.8 0.0 copy-start.12
  4.8 0.0 copy-start.6
  4.8 0.0 copy-start.10
  4.8 0.0 copy-start.11
  4.8 17.3 %all-to-all-start = ((bf16[64,10,2,128]{3,2,1,0:T(2,128)(2,1)}), bf16[64,10,2,128]{3,2,1,0:T(2,128)(2,1)S(1)}, u32[]{:S(2)}, u32[]{:S(2)}) async-start(bf16[64,10,2,128]{3,2,1,0:T(2,128)(2,1)} %bitcast.1), calls=%async_computation | async-start | bytes 655360 | tf_op jit(solution)/shard_map/all_to_all | solution.py:439
  22.1 0.0 copy-start.1
  22.1 0.0 copy-done.12
  22.2 0.0 copy-start.13
  22.2 0.1 reshape.36
  22.2 0.0 copy-start.5
  22.3 0.1 copy.19.w_ref
  22.4 0.1 constant_dynamic-slice_fusion
  22.5 0.1 copy.23
  22.7 0.1 reshape.37
  22.7 0.1 copy-done.13
  22.9 0.1 reshape.38
  23.0 0.2 dynamic-slice_reduce_fusion
  23.1 0.0 copy-done.1
  23.1 0.0 copy-start.7
  23.2 0.0 copy-start.8
  23.2 0.0 copy-start.9
  23.2 0.9 %shard_map.140.feat_ref = f32[3,128,256]{2,1,0:T(8,128)S(1)} custom-call(bf16[3,128,256]{2,1,0:T(8,128)(2,1)S(1)} %copy-done.1, f32[3,128,7]{2,1,0:T(8,128)S(1)} %copy.19.w_ref), custom_call_target="tpu_custom_call" | custom-call | bytes 1048576 | tf_op jit(solution)/shard_map/pallas_call | solution.py:409
  24.1 0.1 pad_maximum_fusion.w_ref
  24.1 11.8 %all-to-all-done = bf16[64,10,2,128]{3,2,1,0:T(2,128)(2,1)S(1)} async-done(((bf16[64,10,2,128]{3,2,1,0:T(2,128)(2,1)}), bf16[64,10,2,128]{3,2,1,0:T(2,128)(2,1)S(1)}, u32[]{:S(2)}, u32[]{:S(2)}) %all-to-all-start) | async-done | bytes 327712 | tf_op jit(solution)/shard_map/all_to_all | solution.py:439
  35.9 0.0 copy-done.6
  35.9 0.0 copy-done.10
  35.9 0.0 copy-done.11
  35.9 0.0 copy-done.5
  35.9 0.0 copy-done.7
  35.9 0.0 copy-done.8
  35.9 0.0 copy-done.9
  35.9 2.6 %shard_map.141 = (bf16[320,128]{1,0:T(8,128)(2,1)S(1)}, f32[256,512]{1,0:T(8,128)S(1)}, f32[11,64,128]{2,1,0:T(8,128)S(1)}) custom-call(bf16[1280,128]{1,0:T(8,128)(2,1)S(1)} %bitcast.11, f32[44]{0:T(128)S(1)} %pad_maximum_fusion.w_ref, bf16[256,128]{1,0:T(8,128)(2,1)S(1)} %copy-done.8, bf16[256,128]{1,0:T(8,128)(2,1)S(1)} %copy-done.9, ...), custom_call_target="tpu_custom_call" | custom-call | flops 800000000 | bytes 1048576 | tf_op jit(solution)/shard_map/pallas_call | solution.py:409
  38.6 0.7 collective-permute-start
  39.3 0.0 collective-permute-done.cross_ref
  39.3 3.8 %shard_map.142 = bf16[768,128]{1,0:T(8,128)(2,1)} custom-call(bf16[320,128]{1,0:T(8,128)(2,1)S(1)} %collective-permute-done.cross_ref, f32[256,512]{1,0:T(8,128)S(1)} %get-tuple-element.12.spec_ref, f32[11,64,128]{2,1,0:T(8,128)S(1)} %get-tuple-element.13.kept_ref, f32[44]{0:T(128)S(1)} %pad_maximum_fusion.w_ref, bf16[256,128]{1,0:T(8,128)(2,1)S(1)} %copy-done.8, ...), custom_call_target="tpu_custom_call" | custom-call | flops 800000000 | bytes 1048576 | tf_op jit(solution)/shard_map/pallas_call | solution.py:409
  43.0 14.2 %all-to-all-start.1 = ((bf16[64,6,2,128]{3,2,1,0:T(2,128)(2,1)}), bf16[64,6,2,128]{3,2,1,0:T(2,128)(2,1)S(1)}, u32[]{:S(2)}, u32[]{:S(2)}) async-start(bf16[64,6,2,128]{3,2,1,0:T(2,128)(2,1)} %bitcast.4), calls=%async_computation.1 | async-start | bytes 393216 | tf_op jit(solution)/shard_map/all_to_all | solution.py:439
  57.2 0.0 copy-start.3
  57.2 0.1 copy.21.w_ref
  57.4 0.1 copy.22.skip_ref
  57.5 11.6 %all-to-all-done.1 = bf16[64,6,2,128]{3,2,1,0:T(2,128)(2,1)S(1)} async-done(((bf16[64,6,2,128]{3,2,1,0:T(2,128)(2,1)}), bf16[64,6,2,128]{3,2,1,0:T(2,128)(2,1)S(1)}, u32[]{:S(2)}, u32[]{:S(2)}) %all-to-all-start.1) | async-done | bytes 196640 | tf_op jit(solution)/shard_map/all_to_all | solution.py:439
  69.1 0.0 copy-done.3
  69.1 2.9 %shard_map.143 = (f32[128,256]{1,0:T(8,128)}, f32[3,128,256]{2,1,0:T(8,128)}, f32[8,256]{1,0:T(8,128)}) custom-call(bf16[768,128]{1,0:T(8,128)(2,1)S(1)} %bitcast.10, s32[1]{0:T(128)} %bitcast.member_ref, f32[3,128,256]{2,1,0:T(8,128)S(1)} %shard_map.140.feat_ref, f32[3,128,7]{2,1,0:T(8,128)S(1)} %copy.21.w_ref, f32[128,1]{1,0:T(8,128)S(1)} %copy.22.skip_ref, ...), custom_call_target="tpu_custom_call" | custom-call | bytes 1048576 | tf_op jit(solution)/shard_map/pallas_call | solution.py:409
Async XLA Ops:
  0.6 0.9 %copy-start = (bf16[3,128,256]{2,1,0:T(8,128)(2,1)S(1)}, bf16[3,128,256]{2,1,0:T(8,128)(2,1)}, u32[]{:S(2)}) copy-start(bf16[3,128,256]{2,1,0:T(8,128)(2,1)} %x_ref.1) | copy-start | bytes 589828
  1.6 0.9 %copy-start.2 = (f32[128,256]{1,0:T(8,128)S(1)}, f32[128,256]{1,0:T(8,128)}, u32[]{:S(2)}) copy-start(f32[128,256]{1,0:T(8,128)} %cot_ref.1) | copy-start | bytes 393220
  2.5 0.7 copy-start.4
  4.8 17.4 %copy-start.12 = (f32[3,128,7]{1,2,0:T(8,128)S(1)}, f32[3,128,7]{1,2,0:T(8,128)}, u32[]{:S(2)}) copy-start(f32[3,128,7]{1,2,0:T(8,128)} %param.13) | copy-start | bytes 32260
  4.8 31.1 %copy-start.6 = (bf16[512,512]{1,0:T(8,128)(2,1)S(1)}, bf16[512,512]{1,0:T(8,128)(2,1)}, u32[]{:S(2)}) copy-start(bf16[512,512]{1,0:T(8,128)(2,1)} %constant.58.clone.inner_lo) | copy-start | bytes 1572868
  4.8 31.1 %copy-start.10 = (bf16[128,256]{1,0:T(8,128)(2,1)S(1)}, bf16[128,256]{1,0:T(8,128)(2,1)}, u32[]{:S(2)}) copy-start(bf16[128,256]{1,0:T(8,128)(2,1)} %constant.54.clone.back_hi) | copy-start | bytes 196612
  4.8 31.1 %copy-start.11 = (bf16[128,256]{1,0:T(8,128)(2,1)S(1)}, bf16[128,256]{1,0:T(8,128)(2,1)}, u32[]{:S(2)}) copy-start(bf16[128,256]{1,0:T(8,128)(2,1)} %constant.55.clone.back_lo) | copy-start | bytes 196612
  4.8 31.1 %all-to-all-start = ((bf16[64,10,2,128]{3,2,1,0:T(2,128)(2,1)}), bf16[64,10,2,128]{3,2,1,0:T(2,128)(2,1)S(1)}, u32[]{:S(2)}, u32[]{:S(2)}) async-start(bf16[64,10,2,128]{3,2,1,0:T(2,128)(2,1)} %bitcast.1), calls=%async_computation | async-start | bytes 655360 | tf_op jit(solution)/shard_map/all_to_all | solution.py:439
  22.1 1.0 %copy-start.1 = (bf16[3,128,256]{2,1,0:T(8,128)(2,1)S(1)}, bf16[3,128,256]{2,1,0:T(8,128)(2,1)}, u32[]{:S(2)}) copy-start(bf16[3,128,256]{2,1,0:T(8,128)(2,1)} %x_ref.1) | copy-start | bytes 589828
  22.2 0.7 copy-start.13
  22.2 13.7 %copy-start.5 = (bf16[512,512]{1,0:T(8,128)(2,1)S(1)}, bf16[512,512]{1,0:T(8,128)(2,1)}, u32[]{:S(2)}) copy-start(bf16[512,512]{1,0:T(8,128)(2,1)} %constant.57.clone.inner_hi) | copy-start | bytes 1572868
  23.1 12.8 %copy-start.7 = (f32[2,128,256]{2,1,0:T(8,128)S(1)}, f32[2,128,256]{2,1,0:T(8,128)}, u32[]{:S(2)}) copy-start(f32[2,128,256]{2,1,0:T(8,128)} %constant.56.clone.twiddle) | copy-start | bytes 786436
  23.2 12.8 %copy-start.8 = (bf16[256,128]{1,0:T(8,128)(2,1)S(1)}, bf16[256,128]{1,0:T(8,128)(2,1)}, u32[]{:S(2)}) copy-start(bf16[256,128]{1,0:T(8,128)(2,1)} %constant.52.clone.outer_hi) | copy-start | bytes 196612
  23.2 12.8 %copy-start.9 = (bf16[256,128]{1,0:T(8,128)(2,1)S(1)}, bf16[256,128]{1,0:T(8,128)(2,1)}, u32[]{:S(2)}) copy-start(bf16[256,128]{1,0:T(8,128)(2,1)} %constant.53.clone.outer_lo) | copy-start | bytes 196612
  38.6 0.7 collective-permute-start
  43.0 26.0 %all-to-all-start.1 = ((bf16[64,6,2,128]{3,2,1,0:T(2,128)(2,1)}), bf16[64,6,2,128]{3,2,1,0:T(2,128)(2,1)S(1)}, u32[]{:S(2)}, u32[]{:S(2)}) async-start(bf16[64,6,2,128]{3,2,1,0:T(2,128)(2,1)} %bitcast.4), calls=%async_computation.1 | async-start | bytes 393216 | tf_op jit(solution)/shard_map/all_to_all | solution.py:439
  57.2 11.9 %copy-start.3 = (f32[128,256]{1,0:T(8,128)S(1)}, f32[128,256]{1,0:T(8,128)}, u32[]{:S(2)}) copy-start(f32[128,256]{1,0:T(8,128)} %cot_ref.1) | copy-start | bytes 393220

commit v2 on v1

v2 whole, which is shorter than its diff:
```python
import functools
import math

import jax
import jax.numpy as jnp
import ml_dtypes
import numpy as np
from jax import lax
from jax.experimental import pallas as pl
from jax.experimental.pallas import tpu as pltpu
from jax.sharding import PartitionSpec as P

BF16 = jnp.bfloat16
F32 = jnp.float32
LANES = 128
TAPS = 7
IN_PROD, IN_MIXED, IN_FILT, IN_RIM, IN_ROWS = 0, 4, 8, 10, 12
CROSS_FILT, CROSS_GRAD, CROSS_TOPS, CROSS_ROWS = 0, 2, 4, 5
OUT_LONG, OUT_GRAD, OUT_FILT, OUT_RIM, OUT_HEAD, OUT_ROWS = 0, 4, 8, 10, 11, 12
RIM = TAPS - 1
COT_LANE = 12 * RIM
IN_TOP_LANE = 16 * RIM
TOP_LANE = 12 * RIM
REACH = 125.0
TABLES = 7


def halves(array):
    array = np.asarray(array, np.float32)
    high = array.astype(ml_dtypes.bfloat16)
    low = (array - high.astype(np.float32)).astype(ml_dtypes.bfloat16)
    return high, low


@functools.lru_cache(maxsize=None)
def tables(pieces, length, scale):
    blocks = 2 * pieces
    total = blocks * length
    freq = np.arange(blocks)[:, None]
    angle = 2.0 * np.pi * ((freq * np.arange(pieces)[None, :]) % blocks) / blocks
    cos, sin = np.cos(angle), np.sin(angle)
    outer = np.block([[cos, sin], [-sin, cos]])
    back = np.block([[cos.T, sin.T], [sin.T, -cos.T]]) * (scale / total)
    angle = 2.0 * np.pi * ((freq * np.arange(length)[None, :]) % total) / total
    twiddle = np.stack([np.cos(angle), -np.sin(angle)]).astype(np.float32)
    angle = 2.0 * np.pi * np.arange(length // 2) / length
    middle = np.zeros((2, 8, length), np.float32)
    middle[:, 0, : length // 2] = np.stack([np.cos(angle), -np.sin(angle)])
    twiddle = np.concatenate([twiddle, middle], axis=1)
    count = np.arange(length // 2)
    angle = 2.0 * np.pi * ((count[:, None] * count[None, :]) % (length // 2)) / (length // 2)
    cos, sin = np.cos(angle), np.sin(angle)
    inner = np.block([[cos, -sin], [sin, cos]])
    return (*halves(outer), *halves(back), twiddle, *halves(inner))


def split(value):
    high = value.astype(BF16)
    return high, (value - high.astype(F32)).astype(BF16)


def product3(left, right):
    left = jnp.concatenate([left[0], left[1], left[0]], axis=1)
    right = jnp.concatenate([right[0], right[0], right[1]], axis=0)
    return jnp.dot(left, right, preferred_element_type=F32)


def encoded(value):
    top = jnp.max(jnp.abs(value), axis=1, keepdims=True)
    top = (jnp.maximum(top, 1e-30) * 1.008).astype(BF16).astype(F32)
    square = jnp.abs(value) * (1.0 / top)
    size = square * lax.rsqrt(jnp.maximum(square, 1e-30))
    code = jnp.exp2(size * (2.0 * REACH) - REACH)
    return jnp.where(value < 0.0, -code, code), top


def decoded(code, top):
    size = (jnp.log2(jnp.abs(code)) + REACH) * (0.5 / REACH)
    value = size * size * top
    return jnp.where(code < 0.0, -value, value)


class Lines:
    def __init__(self, ref, rows):
        self.ref, self.rows = ref, rows
        self.count = ref.shape[0] // rows

    def get(self, row):
        return self.ref[pl.ds(row, self.count, stride=self.rows), :]

    def put(self, row, value):
        self.ref[pl.ds(row, self.count, stride=self.rows), :] = value

    def get_block(self, row):
        return jnp.concatenate([self.get(row), self.get(row + 1)], axis=1)

    def put_block(self, row, value):
        self.put(row, value[:, :LANES])
        self.put(row + 1, value[:, LANES:])


def in_lanes(columns, first, like):
    lane = lax.broadcasted_iota(jnp.int32, like.shape, 1)
    for place, column in enumerate(columns):
        like = jnp.where(lane == first + place, column, like)
    return like


def exchanged(value, member, owners):
    size = value.shape[0] // owners
    step = 1
    while step < owners:
        order = [place ^ step for place in range(owners)]
        swapped = jnp.concatenate([value[k * size : (k + 1) * size] for k in order], axis=0)
        value = jnp.where((member & step) != 0, swapped, value)
        step *= 2
    return value


def rolled(value, lanes):
    lanes %= value.shape[1]
    return pltpu.roll(value, lanes, 1) if lanes else value


def lane_numbers(like):
    return lax.broadcasted_iota(jnp.int32, like.shape, 1)


def put_lanes(target, first, count, value, start=0):
    lane = lane_numbers(target)
    inside = (lane >= first) & (lane < first + count)
    return jnp.where(inside, rolled(value, first - start), target)


def eight_rows(taps):
    return jnp.concatenate([taps, jnp.zeros((8 - TAPS, taps.shape[1]), F32)], axis=0)


def spread_taps(taps):
    columns = jnp.transpose(eight_rows(taps))
    shape = (columns.shape[0], LANES)
    return jnp.concatenate(
        [jnp.broadcast_to(columns[:, tap : tap + 1], shape) for tap in range(TAPS)], axis=1
    )


def inner_featured(signal, spread):
    halves_total = [0.0, 0.0]
    for offset in range(TAPS):
        shifted = pltpu.roll(signal, offset, 1) if offset else signal
        weight = spread[:, offset * LANES : (offset + 1) * LANES]
        for half in range(2):
            part = weight * shifted[:, half * LANES : (half + 1) * LANES]
            halves_total[half] = halves_total[half] + part if offset else part
    return jnp.concatenate(halves_total, axis=1)


def own_lanes(taps_ref, skip, group):
    lane = lax.broadcasted_iota(jnp.int32, (8, LANES), 1)
    row = lax.broadcasted_iota(jnp.int32, (8, LANES), 0)
    pieces = LANES // 2
    own = jnp.zeros((8, LANES), F32)
    skips = jnp.broadcast_to(skip, (8, LANES))
    for side in range(2):
        here = lane == group + side * pieces
        value = jnp.sum(jnp.where(here, skips, 0.0), axis=1, keepdims=True)
        first = 2 * RIM * side
        own = jnp.where((row == TAPS) & (lane >= first) & (lane < first + RIM), value, own)
        for stream in range(3):
            value = jnp.sum(
                jnp.where(here, eight_rows(taps_ref[stream]), 0.0), axis=1, keepdims=True
            )
            first = 2 * RIM * (stream * 2 + side)
            own = jnp.where((row < TAPS) & (lane >= first) & (lane < first + RIM), value, own)
    return own


def pack_kernel(
    owners,
    place_ref,
    x_hbm,
    cot_hbm,
    filt_hbm,
    w_hbm,
    skip_hbm,
    out_ref,
    own_ref,
    scratch,
    x_ref,
    cot_ref,
    filt_ref,
    w_ref,
    skip_ref,
    spread_ref,
    sems,
):
    copies = [
        pltpu.make_async_copy(source, target, sems.at[place])
        for place, (source, target) in enumerate(
            [
                (w_hbm, w_ref),
                (x_hbm.at[1], x_ref.at[1]),
                (x_hbm.at[2], x_ref.at[2]),
                (x_hbm.at[0], x_ref.at[0]),
                (cot_hbm, cot_ref),
                (filt_hbm, filt_ref),
                (skip_hbm, skip_ref),
            ]
        )
    ]
    for copy in copies:
        copy.start()
    lines = Lines(scratch, IN_ROWS)
    pieces = lines.count
    member = place_ref[0]
    blank = jnp.zeros((pieces, LANES), F32)
    lane = lane_numbers(blank)
    rims = [blank, blank]
    featured = {}

    def inner_part(value):
        return jnp.concatenate(
            [jnp.where(lane < RIM, 0.0, value[:, :LANES]), value[:, LANES:]], axis=1
        )

    copies[0].wait()
    for stream in range(3):
        spread_ref[stream] = spread_taps(w_ref[stream])
    for place, stream in ((1, 1), (2, 2), (3, 0)):
        copies[place].wait()
        for side in range(2):
            rows = slice(side * pieces, (side + 1) * pieces)
            signal = x_ref[stream, rows, :].astype(F32)
            featured[stream, side] = inner_featured(signal, spread_ref[stream, rows, :])
            first = 2 * RIM * (stream * 2 + side)
            rims[side] = put_lanes(rims[side], first, RIM, signal[:, LANES:], LANES - RIM)
            rims[side] = put_lanes(rims[side], first + RIM, RIM, signal[:, :LANES])
    products, mixed = [], []
    for side in range(2):
        products.append(inner_part(featured[1, side] * featured[2, side]))
    copies[4].wait()
    for side in range(2):
        cot = cot_ref[side * pieces : (side + 1) * pieces, :]
        mixed.append(inner_part(featured[0, side] * cot))
        high = cot[:, :LANES].astype(BF16).astype(F32)
        first = COT_LANE + 2 * RIM * side
        rims[side] = put_lanes(rims[side], first, RIM, high)
        rims[side] = put_lanes(rims[side], first + RIM, RIM, cot[:, :LANES] - high)
    tops = []
    for row, values in ((IN_PROD, products), (IN_MIXED, mixed)):
        for side in range(2):
            code, top = encoded(exchanged(values[side], member, owners))
            lines.put_block(row + 2 * side, code)
            tops.append(top)
    copies[5].wait()
    code, top = encoded(filt_ref[...])
    lines.put_block(IN_FILT, jnp.concatenate([code] * owners, axis=0))
    tops.append(jnp.concatenate([top] * owners, axis=0))
    rim = exchanged(rims[0] + rims[1], member, owners)
    lines.put(IN_RIM, in_lanes(tops, IN_TOP_LANE, rim))
    lines.put(IN_RIM + 1, blank)
    out_ref[...] = scratch[...].astype(BF16)
    copies[6].wait()
    own_ref[...] = own_lanes(w_ref, skip_ref[...], place_ref[1])


def turned(re, im, twiddle):
    turn_re, turn_im = twiddle
    return re * turn_re - im * turn_im, re * turn_im + im * turn_re


def parted(re, im, middle):
    half = re.shape[1] // 2
    even = jnp.concatenate([re[:, :half] + re[:, half:], im[:, :half] + im[:, half:]], axis=1)
    odd = turned(re[:, :half] - re[:, half:], im[:, :half] - im[:, half:], middle)
    return jnp.concatenate([even, jnp.concatenate(odd, axis=1)], axis=0)


def joined(pair, middle):
    count, half = pair.shape[0] // 2, pair.shape[1] // 2
    re, im = pair[:count, :half], pair[:count, half:]
    turn_re, turn_im = turned(pair[count:, :half], pair[count:, half:], middle)
    whole_re = jnp.concatenate([re + turn_re, re - turn_re], axis=1)
    return whole_re, jnp.concatenate([im + turn_im, im - turn_im], axis=1)


def spectrum(columns, twiddle, middle, count):
    re, im = turned(columns[:count], columns[count:], twiddle)
    return parted(re, im, middle)


def upright(spectra, inner, twiddle, middle, count):
    inside = product3(split(spectra), inner)
    columns = []
    for start in range(0, spectra.shape[0], 2 * count):
        re, im = joined(inside[start : start + 2 * count], middle)
        columns.append(jnp.concatenate(turned(re, im, twiddle), axis=0))
    return jnp.concatenate(columns, axis=1)


def halved_lanes(value):
    high = value.astype(BF16).astype(F32)
    lane = lane_numbers(value)
    both = jnp.where(lane % (2 * RIM) < RIM, high, rolled(value - high, RIM))
    return jnp.where(lane < 12 * RIM, both, 0.0)


def forward_kernel(
    r_ref,
    w_ref,
    outer_hi,
    outer_lo,
    back_hi,
    back_lo,
    twiddle_ref,
    inner_hi,
    inner_lo,
    cross_ref,
    spec_ref,
    kept_ref,
    scratch,
    cross_scratch,
):
    scratch[...] = r_ref[...].astype(F32)
    lines = Lines(scratch, IN_ROWS)
    cross = Lines(cross_scratch, CROSS_ROWS)
    pieces = lines.count
    count = 2 * pieces
    length = 2 * LANES
    rim = lines.get(IN_RIM)
    tops = [rim[:, IN_TOP_LANE + place : IN_TOP_LANE + place + 1] for place in range(5)]
    lane = lane_numbers(rim)
    row_number = lax.broadcasted_iota(jnp.int32, rim.shape, 0)
    before = jnp.where(row_number == 0, 0.0, pltpu.roll(rim, 1, 0))
    ends = jnp.where(lane % (2 * RIM) < RIM, before, rim)
    head = jnp.zeros_like(rim)
    for offset in range(TAPS):
        head = head + w_ref[offset : offset + 1, :] * rolled(ends, offset - RIM)
    side_lanes = 2 * RIM
    head_key, head_value = rolled(head, -2 * side_lanes), rolled(head, -4 * side_lanes)
    head_cot = rolled(rim + rolled(rim, -RIM), -COT_LANE)
    head_prod, head_mixed = head_key * head_value, head_cot * head
    for place, array in enumerate((head, head_prod, head_mixed, head_key, head_value, head_cot)):
        kept_ref[place] = array

    def whole(row, top, first):
        value = decoded(lines.get_block(row), top)
        return jnp.concatenate([jnp.where(lane < RIM, first, value[:, :LANES]), value[:, LANES:]], axis=1)

    prod, mixed = [], []
    for side in range(2):
        shift = -side_lanes * side
        prod.append(whole(IN_PROD + 2 * side, tops[side], rolled(head_prod, shift)))
        mixed.append(whole(IN_MIXED + 2 * side, tops[2 + side], rolled(head_mixed, shift)))

    signals = jnp.concatenate(
        [jnp.concatenate(prod, axis=0), jnp.concatenate(mixed, axis=0)], axis=1
    )
    twiddle = (twiddle_ref[0, :count], twiddle_ref[1, :count])
    middle = tuple(twiddle_ref[place, count : count + 1, :LANES] for place in range(2))
    spread = product3((outer_hi[...], outer_lo[...]), split(signals))
    parts = [
        spectrum(spread[:, start : start + length], twiddle, middle, count) for start in (0, length)
    ]
    inner = (inner_hi[...], inner_lo[...])
    spectra = product3(split(jnp.concatenate(parts, axis=0)), inner)
    spec_ref[...] = spectra
    z_re, z_im = spectra[:length, :LANES], spectra[:length, LANES:]
    m_re, m_im = spectra[length:, :LANES], spectra[length:, LANES:]
    tail = jnp.concatenate([z_re * m_re + z_im * m_im, z_im * m_re - z_re * m_im], axis=1)
    columns = upright(tail, inner, twiddle, middle, count)
    partial = product3((back_hi[:pieces, :], back_lo[:pieces, :]), split(columns))
    code, top = encoded(partial)
    cross.put_block(CROSS_GRAD, code)
    cross.put_block(CROSS_FILT, lines.get_block(IN_FILT))
    blank = jnp.zeros((pieces, LANES), F32)
    cross.put(CROSS_TOPS, in_lanes([tops[4], top], 0, blank))
    cross_ref[...] = cross_scratch[...].astype(BF16)


def inverse_kernel(
    cross_ref,
    spec_ref,
    kept_ref,
    w_ref,
    outer_hi,
    outer_lo,
    back_hi,
    back_lo,
    twiddle_ref,
    inner_hi,
    inner_lo,
    out_ref,
    cross_scratch,
    scratch,
):
    cross_scratch[...] = cross_ref[...].astype(F32)
    cross = Lines(cross_scratch, CROSS_ROWS)
    lines = Lines(scratch, OUT_ROWS)
    pieces = lines.count
    count = 2 * pieces
    length = 2 * LANES
    tops = cross.get(CROSS_TOPS)
    filt = decoded(cross.get_block(CROSS_FILT), tops[:, 0:1])
    inner = (inner_hi[...], inner_lo[...])
    twiddle = (twiddle_ref[0, :count], twiddle_ref[1, :count])
    middle = tuple(twiddle_ref[place, count : count + 1, :LANES] for place in range(2))
    spread = product3((outer_hi[:, :pieces], outer_lo[:, :pieces]), split(filt))
    spectra = product3(split(spectrum(spread, twiddle, middle, count)), inner)
    f_re, f_im = spectra[:, :LANES], spectra[:, LANES:]
    z_re, z_im = spec_ref[:length, :LANES], spec_ref[:length, LANES:]
    m_re, m_im = spec_ref[length:, :LANES], spec_ref[length:, LANES:]
    long_pair = jnp.concatenate(
        [z_re * f_re - z_im * f_im, -(z_re * f_im + z_im * f_re)], axis=1
    )
    grad_pair = jnp.concatenate([m_re * f_re + m_im * f_im, m_re * f_im - m_im * f_re], axis=1)
    columns = upright(
        jnp.concatenate([long_pair, grad_pair], axis=0), inner, twiddle, middle, count
    )
    restored = product3((back_hi[...], back_lo[...]), split(columns))
    side_lanes = 2 * RIM
    blank = jnp.zeros((pieces, LANES), F32)
    heads = {OUT_LONG: blank, OUT_GRAD: blank}
    out_tops = []
    for row, columns in ((OUT_LONG, slice(0, length)), (OUT_GRAD, slice(length, 2 * length))):
        for side in range(2):
            value = restored[side * pieces : (side + 1) * pieces, columns]
            code, top = encoded(value)
            lines.put_block(row + 2 * side, code)
            out_tops.append(top)
            heads[row] = put_lanes(heads[row], side_lanes * side, RIM, value[:, :LANES])
    head, prod, mixed, key, value, cot = [kept_ref[place] for place in range(6)]
    skip = w_ref[TAPS : TAPS + 1, :]
    grad_query = cot * (heads[OUT_LONG] + skip * prod)
    grad_product = heads[OUT_GRAD] + skip * mixed
    rim = put_lanes(blank, 0, 2 * side_lanes, grad_query)
    rim = put_lanes(rim, 2 * side_lanes, 2 * side_lanes, grad_product * value)
    rim = put_lanes(rim, 4 * side_lanes, 2 * side_lanes, grad_product * key)
    row_number = lax.broadcasted_iota(jnp.int32, rim.shape, 0)
    rim = jnp.where(row_number == pieces - 1, 0.0, pltpu.roll(rim, pieces - 1, 0))
    lines.put_block(OUT_FILT, cross.get_block(CROSS_GRAD))
    lines.put(OUT_RIM, in_lanes([*out_tops, tops[:, 1:2]], TOP_LANE, halved_lanes(rim)))
    lines.put(OUT_HEAD, halved_lanes(head))
    out_ref[...] = scratch[...].astype(BF16)


def feature_kernel(*refs):
    x_hbm, w_hbm, skip_hbm = refs[:3]
    out_ref, spread_ref, wide_ref = refs[3 + TABLES : 6 + TABLES]
    x_ref, w_ref, skip_ref, sems = refs[6 + 2 * TABLES :]
    pairs = [(w_hbm, w_ref), (x_hbm, x_ref), (skip_hbm, skip_ref)]
    pairs += list(zip(refs[3 : 3 + TABLES], refs[6 + TABLES : 6 + 2 * TABLES]))
    copies = [
        pltpu.make_async_copy(source, target, sems.at[place])
        for place, (source, target) in enumerate(pairs)
    ]
    for copy in copies:
        copy.start()
    copies[0].wait()
    for stream in range(3):
        spread_ref[stream] = spread_taps(w_ref[stream])
    copies[1].wait()
    for stream in range(3):
        out_ref[stream] = inner_featured(x_ref[stream].astype(F32), spread_ref[stream])
    copies[2].wait()
    column = jnp.transpose(jnp.broadcast_to(skip_ref[...], (8, LANES)))[:, 0:1]
    wide_ref[...] = jnp.broadcast_to(column, wide_ref.shape)
    for copy in copies[3:]:
        copy.wait()


def local_kernel(
    owners,
    r_ref,
    place_ref,
    feat_ref,
    w_ref,
    skip_ref,
    cot_ref,
    out_ref,
    grad_ref,
    tail_ref,
    scratch,
    out_room,
    grad_room,
    tail_room,
    sems,
):
    member = place_ref[0]
    scratch[...] = r_ref[...].astype(F32)
    lines = Lines(scratch, OUT_ROWS)
    pieces = lines.count
    copies = []

    def send(source, target):
        copy = pltpu.make_async_copy(source, target, sems.at[len(copies)])
        copy.start()
        copies.append(copy)

    def block(row, top_place):
        return decoded(lines.get_block(row), tops[:, TOP_LANE + top_place : TOP_LANE + top_place + 1])

    tops = lines.get(OUT_RIM)
    rim = exchanged(tops, member, owners)
    rim = rim + pltpu.roll(rim, LANES - RIM, 1)
    head = exchanged(lines.get(OUT_HEAD), member, owners)
    head = head + pltpu.roll(head, LANES - RIM, 1)
    lane = lax.broadcasted_iota(jnp.int32, (pieces, LANES), 1)

    def first_lanes(array, place):
        return rolled(array, -2 * RIM * place)

    for side in range(2):
        rows = slice(side * pieces, (side + 1) * pieces)
        featured = []
        for stream in range(3):
            inside = feat_ref[stream, rows, :]
            left = first_lanes(head, stream * 2 + side)
            left = jnp.where(lane < RIM, left, inside[:, :LANES])
            featured.append(jnp.concatenate([left, inside[:, LANES:]], axis=1))
        query, key, value = featured
        cot = cot_ref[rows, :]
        skip = jnp.concatenate([skip_ref[rows, :]] * 2, axis=1)
        long_out = exchanged(block(OUT_LONG + 2 * side, side), member, owners)
        mixer = long_out + skip * (key * value)
        out_room[rows, :] = query * mixer
        send(out_room.at[rows, :], out_ref.at[rows, :])
        grad_long = exchanged(block(OUT_GRAD + 2 * side, 2 + side), member, owners)
        grad_product = grad_long + skip * (cot * query)
        for stream, grad in enumerate((cot * mixer, grad_product * value, grad_product * key)):
            after = first_lanes(rim, stream * 2 + side)
            near, far = grad[:, :LANES], grad[:, LANES:]
            weight = w_ref[stream, rows, :LANES]
            total_near, total_far = weight * near, weight * far
            for offset in range(1, TAPS):
                weight = w_ref[stream, rows, offset * LANES : (offset + 1) * LANES]
                wrapped = lane < offset
                total_near = total_near + weight * rolled(jnp.where(wrapped, far, near), -offset)
                total_far = total_far + weight * rolled(jnp.where(wrapped, after, far), -offset)
            grad_room[stream, rows, :LANES] = total_near
            grad_room[stream, rows, LANES:] = total_far
            send(grad_room.at[stream, rows, :], grad_ref.at[stream, rows, :])
    partial = block(OUT_FILT, 4)
    owned = pieces // owners
    total = partial[:owned]
    for place in range(1, owners):
        total = total + partial[place * owned : (place + 1) * owned]
    tail_room[...] = total
    send(tail_room, tail_ref)
    for copy in copies:
        copy.wait()


VMEM_SPEC = pl.BlockSpec(memory_space=pltpu.VMEM)
SMEM_SPEC = pl.BlockSpec(memory_space=pltpu.SMEM)
ANY_SPEC = pl.BlockSpec(memory_space=pl.ANY)
HBM_SPEC = pl.BlockSpec(memory_space=pltpu.HBM)


def call(
    kernel, out_shape, operands, scratch=(), specs=None, flops=0, out_spec=VMEM_SPEC, room_mib=24
):
    specs = specs or {}
    return pl.pallas_call(
        kernel,
        out_shape=out_shape,
        in_specs=[specs.get(place, VMEM_SPEC) for place in range(len(operands))],
        out_specs=jax.tree.map(lambda _: out_spec, out_shape),
        scratch_shapes=list(scratch),
        compiler_params=pltpu.CompilerParams(vmem_limit_bytes=room_mib << 20),
        cost_estimate=pl.CostEstimate(flops=flops, bytes_accessed=1 << 20, transcendentals=0),
    )(*operands)


def shards(inputs, short_weight, skip, filters, cotangent):
    pieces = lax.axis_size("ctx")
    owners = lax.axis_size("ch")
    position = lax.axis_index("ctx")
    member = lax.axis_index("ch")
    _, channels, length = inputs.shape
    owned = filters.shape[0]
    count = 2 * pieces
    scale = 1.0 / math.sqrt(pieces * length)

    def shape(*dims, dtype=F32):
        return jax.ShapeDtypeStruct(dims, dtype)

    def pinned(array):
        return pltpu.with_memory_space_constraint(array, pltpu.HBM)

    def room(rows):
        return pltpu.VMEM((pieces * rows, LANES), F32)

    def transposed(array):
        rows = array.shape[0] // pieces
        array = lax.all_to_all(array.reshape(pieces, rows // 2, 2, LANES), "ctx", 0, 0)
        return array.reshape(pieces * rows, LANES)

    group = ((position // owned) ^ member) * owned + position % owned
    place = jnp.stack([member, group]).astype(jnp.int32)
    taps = jnp.transpose(short_weight, (0, 2, 1))
    skip_row = skip[None]
    sent, own = call(
        functools.partial(pack_kernel, owners),
        (shape(pieces * IN_ROWS, LANES, dtype=BF16), shape(8, LANES)),
        (place, *(pinned(array) for array in (inputs, cotangent, filters, taps, skip_row))),
        [
            room(IN_ROWS),
            pltpu.VMEM(inputs.shape, BF16),
            pltpu.VMEM(cotangent.shape, F32),
            pltpu.VMEM(filters.shape, F32),
            pltpu.VMEM(taps.shape, F32),
            pltpu.VMEM(skip_row.shape, F32),
            pltpu.VMEM((3, channels, TAPS * LANES), F32),
            pltpu.SemaphoreType.DMA((7,)),
        ],
        specs={0: SMEM_SPEC, **{operand: HBM_SPEC for operand in range(1, 6)}},
    )
    received = transposed(sent)
    constants = [jnp.asarray(table) for table in tables(pieces, length, scale)]
    beside = call(
        feature_kernel,
        (
            shape(3, channels, length),
            shape(3, channels, TAPS * LANES),
            shape(channels, LANES),
            *(shape(*table.shape, dtype=table.dtype) for table in constants),
        ),
        [pinned(array) for array in (inputs, taps, skip_row, *constants)],
        [
            *(pltpu.VMEM(array.shape, array.dtype) for array in (inputs, taps, skip_row)),
            pltpu.SemaphoreType.DMA((3 + TABLES,)),
        ],
        specs={operand: HBM_SPEC for operand in range(3 + TABLES)},
        flops=10000000,
    )
    received, beside = lax.optimization_barrier((received, beside))
    beside, constants = beside[:3], beside[3:]
    cross, spectra, kept = call(
        forward_kernel,
        (
            shape(pieces * CROSS_ROWS, LANES, dtype=BF16),
            shape(2 * length, length),
            shape(6, pieces, LANES),
        ),
        (received, own, *constants),
        [room(IN_ROWS), room(CROSS_ROWS)],
        flops=800000000,
    )
    partners = [
        (place * owners + shard, place * owners + (shard ^ (place // owned)))
        for place in range(pieces)
        for shard in range(owners)
    ]
    cross = lax.ppermute(cross, ("ctx", "ch"), partners)
    sent = call(
        inverse_kernel,
        shape(pieces * OUT_ROWS, LANES, dtype=BF16),
        (cross, spectra, kept, own, *constants),
        [room(CROSS_ROWS), room(OUT_ROWS)],
        flops=800000000,
    )
    received = transposed(sent)

    return call(
        functools.partial(local_kernel, owners),
        (shape(channels, length), shape(3, channels, length), shape(owned, length)),
        (received, place, *beside, cotangent),
        [
            room(OUT_ROWS),
            pltpu.VMEM((channels, length), F32),
            pltpu.VMEM((3, channels, length), F32),
            pltpu.VMEM((owned, length), F32),
            pltpu.SemaphoreType.DMA((9,)),
        ],
        specs={1: SMEM_SPEC},
        out_spec=ANY_SPEC,
    )


def solution(mesh):
    in_specs = (P(None, "ch", "ctx"), P(None, "ch", None), P("ch"), P("ch", "ctx"), P("ch", "ctx"))
    out_specs = (P("ch", "ctx"), P(None, "ch", "ctx"), P("ch", "ctx"))
    return jax.shard_map(shards, mesh=mesh, in_specs=in_specs, out_specs=out_specs, check_vma=False)
```

time: 72.8 us -> 65.5 us (0.90)
  blocking collectives: 0 us -> 24.9 us
  starting transfers between devices: 32.1 us -> 17.8 us
  waiting for transfers between devices: 23.4 us -> 9.75 us
  local copies, waits for them, and re-layouts: 3.75 us -> 0.01 us
    all_to_all x0 -> x1, blocking collectives: none -> 24.9 us  [transposed(): lax.all_to_all(array.reshape(pieces, rows // 2, 2, LANES), 'ctx', 0, 0)]
    all_to_all x2 -> x1, starting transfers between devices: 31.4 us -> 17.1 us  [transposed(): lax.all_to_all(array.reshape(pieces, rows // 2, 2, LANES), 'ctx', 0, 0)]
    all_to_all x2 -> x1, waiting for transfers between devices: 23.4 us -> 9.74 us  [transposed(): lax.all_to_all(array.reshape(pieces, rows // 2, 2, LANES), 'ctx', 0, 0)]
    unnamed x30 -> x2, local copies, waits for them, and re-layouts: 2.98 us -> 0.01 us
  transfers between devices with their start and end apart: 3 -> 2, of which waited for: 2 -> 1; matrix products, arithmetic and copies ran while one was open for 2% -> 0% of each run, Pallas kernels for 1% -> 3%
where the time goes in v2:
time: 65.5 us; the launch traced here: 64.8 us
  blocking collectives  24.9 us (38%)
  starting transfers between devices  17.8 us (27%)
  Pallas kernels  11.5 us (18%)
  waiting for transfers between devices  9.75 us (15%)
  between operations  0.71 us (1%)
    all_to_all x1, blocking collectives, transposed(): lax.all_to_all(array.reshape(pieces, rows // 2, 2, LANES), 'ctx', 0, 0)  24.9 us
    all_to_all x1, starting transfers between devices, transposed(): lax.all_to_all(array.reshape(pieces, rows // 2, 2, LANES), 'ctx', 0, 0)  17.1 us
    pallas_call x5, Pallas kernels, call(): pl.pallas_call(kernel, out_shape=out_shape, in_specs=[specs.get(place, VM...  11.5 us
    all_to_all x1, waiting for transfers between devices, transposed(): lax.all_to_all(array.reshape(pieces, rows // 2, 2, LANES), 'ctx', 0, 0)  9.74 us
  transfers between devices with their start and end apart: 2, of which 1 were waited for; matrix products, arithmetic and copies ran while one was open for 0% of the time, Pallas kernels for 3%

profile of v2, /device:TPU:1, one launch (start us, length us, event | category | flops | bytes accessed | tf_op | source)
XLA Modules:
  0.0 64.8 jit_solution(15616567719274153808)
XLA Ops:
  0.7 0.1 pad_add_fusion.place_ref
  0.7 3.6 %shard_map.139 = (bf16[768,128]{1,0:T(8,128)(2,1)}, f32[8,128]{1,0:T(8,128)S(1)}) custom-call(s32[2]{0:T(128)S(1)} %pad_add_fusion.place_ref, bf16[3,128,256]{2,1,0:T(8,128)(2,1)} %refs_0_.1, f32[128,256]{1,0:T(8,128)} %cot_ref.1, f32[8,256]{1,0:T(8,128)} %filt_hbm.1, f32[3,7,128]{2,1,0:T(8,128)} %bitcast.11, f32[1,128]{1,0:T(1,128)} %bitcast.13), custom_call_target="tpu_custom_call" | custom-call | bytes 1048576 | tf_op jit(solution)/shard_map/pallas_call | solution.py:564
  4.4 17.1 %all-to-all-start = ((bf16[64,6,2,128]{3,2,1,0:T(2,128)(2,1)}), bf16[64,6,2,128]{3,2,1,0:T(2,128)(2,1)S(1)}, u32[]{:S(2)}, u32[]{:S(2)}) async-start(bf16[64,6,2,128]{3,2,1,0:T(2,128)(2,1)} %bitcast.4), calls=%async_computation | async-start | bytes 393216 | tf_op jit(solution)/shard_map/all_to_all | solution.py:596
  21.5 2.1 %shard_map.140 = (f32[3,128,256]{2,1,0:T(8,128)S(1)}, f32[3,128,896]{2,1,0:T(8,128)S(1)}, f32[128,128]{1,0:T(8,128)S(1)}, bf16[256,128]{1,0:T(8,128)(2,1)S(1)}, ...) custom-call(bf16[3,128,256]{2,1,0:T(8,128)(2,1)} %refs_0_.1, ...), custom_call_target="tpu_custom_call" | custom-call | flops 10000000 | bytes 1048576 | tf_op jit(solution)/shard_map/pallas_call | solution.py:564
  23.6 9.7 %all-to-all-done = bf16[64,6,2,128]{3,2,1,0:T(2,128)(2,1)S(1)} async-done(((bf16[64,6,2,128]{3,2,1,0:T(2,128)(2,1)}), bf16[64,6,2,128]{3,2,1,0:T(2,128)(2,1)S(1)}, u32[]{:S(2)}, u32[]{:S(2)}) %all-to-all-start) | async-done | bytes 196640 | tf_op jit(solution)/shard_map/all_to_all | solution.py:596
  33.4 1.7 %shard_map.141 = (bf16[320,128]{1,0:T(8,128)(2,1)S(1)}, f32[512,256]{1,0:T(8,128)S(1)}, f32[6,64,128]{2,1,0:T(8,128)S(1)}) custom-call(bf16[768,128]{1,0:T(8,128)(2,1)S(1)} %bitcast.9, f32[8,128]{1,0:T(8,128)S(1)} %get-tuple-element.41.w_ref, bf16[256,128]{1,0:T(8,128)(2,1)S(1)} %get-tuple-element.42.outer_hi, ...), custom_call_target="tpu_custom_call" | custom-call | flops 800000000 | bytes 1048576 | tf_op jit(solution)/shard_map/pallas_call | solution.py:564
  35.1 0.7 %collective-permute-start = (bf16[320,128]{1,0:T(8,128)(2,1)S(1)}, bf16[320,128]{1,0:T(8,128)(2,1)S(1)}, u32[]{:S(2)}, u32[]{:S(2)}) collective-permute-start(bf16[320,128]{1,0:T(8,128)(2,1)S(1)} %get-tuple-element.49), channel_id=1, source_target_pairs={{0,0},{1,1},{2,2},{3,3},{4,4},{5,5},{6,6},{7,7},{8,8},{9,9},{10,10... | collective-permute-start | bytes 245768 | tf_op jit(solution)/shard_map/ppermute | solution.py:655
  35.8 0.0 collective-permute-done.cross_ref
  35.8 0.0 copy-start
  35.8 1.7 %shard_map.142 = bf16[768,128]{1,0:T(8,128)(2,1)S(1)} custom-call(bf16[320,128]{1,0:T(8,128)(2,1)S(1)} %collective-permute-done.cross_ref, f32[512,256]{1,0:T(8,128)S(1)} %get-tuple-element.50.spec_ref, f32[6,64,128]{2,1,0:T(8,128)S(1)} %get-tuple-element.51.kept_ref, f32[8,128]{1,0:T(8,128)S(1)} %get-tuple-element.41.w_ref, ...), custom_call_target="tpu_custom_call" | custom-call | flops 800000000 | bytes 1048576 | tf_op jit(solution)/shard_map/pallas_call | solution.py:564
  37.5 24.9 %all_to_all.10 = bf16[64,6,2,128]{3,2,1,0:T(2,128)(2,1)S(1)} all-to-all(bf16[64,6,2,128]{3,2,1,0:T(2,128)(2,1)S(1)} %bitcast.10), channel_id=1, replica_groups=mesh['ctx'=64,'ch'=8] {'ctx'}, dimensions={0} | all-to-all | bytes 393216 | tf_op jit(solution)/shard_map/all_to_all | solution.py:596
  62.4 0.0 copy-done
  62.4 2.4 %shard_map.143 = (f32[128,256]{1,0:T(8,128)}, f32[3,128,256]{2,1,0:T(8,128)}, f32[8,256]{1,0:T(8,128)}) custom-call(bf16[768,128]{1,0:T(8,128)(2,1)S(1)} %bitcast.8, s32[2]{0:T(128)S(1)} %pad_add_fusion.place_ref, f32[3,128,256]{2,1,0:T(8,128)S(1)} %get-tuple-element.52.feat_ref, f32[3,128,896]{2,1,0:T(8,128)S(1)} %get-tuple-element.53.w_ref, ...), custom_call_target="tpu_custom_call" | custom-call | bytes 1048576 | tf_op jit(solution)/shard_map/pallas_call | solution.py:564
Async XLA Ops:
  4.4 29.0 %all-to-all-start = ((bf16[64,6,2,128]{3,2,1,0:T(2,128)(2,1)}), bf16[64,6,2,128]{3,2,1,0:T(2,128)(2,1)S(1)}, u32[]{:S(2)}, u32[]{:S(2)}) async-start(bf16[64,6,2,128]{3,2,1,0:T(2,128)(2,1)} %bitcast.4), calls=%async_computation | async-start | bytes 393216 | tf_op jit(solution)/shard_map/all_to_all | solution.py:596
  35.1 0.7 %collective-permute-start = (bf16[320,128]{1,0:T(8,128)(2,1)S(1)}, bf16[320,128]{1,0:T(8,128)(2,1)S(1)}, u32[]{:S(2)}, u32[]{:S(2)}) collective-permute-start(bf16[320,128]{1,0:T(8,128)(2,1)S(1)} %get-tuple-element.49), channel_id=1, source_target_pairs={{0,0},{1,1},{2,2},{3,3},{4,4},{5,5},{6,6},{7,7},{8,8},{9,9},{10,10... | collective-permute-start | bytes 245768 | tf_op jit(solution)/shard_map/ppermute | solution.py:655
  35.8 26.6 %copy-start = (f32[128,256]{1,0:T(8,128)S(1)}, f32[128,256]{1,0:T(8,128)}, u32[]{:S(2)}) copy-start(f32[128,256]{1,0:T(8,128)} %cot_ref.1) | copy-start | bytes 393220

commit v3 on v2

--- a/solution.py
+++ b/solution.py
@@ -23,6 +23,7 @@
 TOP_LANE = 12 * RIM
 REACH = 125.0
 TABLES = 7
+CHUNK = 16
 
 
 def halves(array):
@@ -62,7 +63,11 @@
 def product3(left, right):
     left = jnp.concatenate([left[0], left[1], left[0]], axis=1)
     right = jnp.concatenate([right[0], right[0], right[1]], axis=0)
-    return jnp.dot(left, right, preferred_element_type=F32)
+    parts = [
+        jnp.dot(left[start : start + LANES], right, preferred_element_type=F32)
+        for start in range(0, left.shape[0], LANES)
+    ]
+    return jnp.concatenate(parts, axis=0)
 
 
 def encoded(value):
@@ -137,22 +142,30 @@
 
 
 def spread_taps(taps):
-    columns = jnp.transpose(eight_rows(taps))
-    shape = (columns.shape[0], LANES)
-    return jnp.concatenate(
-        [jnp.broadcast_to(columns[:, tap : tap + 1], shape) for tap in range(TAPS)], axis=1
-    )
+    rest = eight_rows(taps)
+    parts = []
+    for _ in range(3):
+        parts.append(rest.astype(BF16).astype(F32))
+        rest = rest - parts[-1]
+    columns = jnp.transpose(jnp.concatenate(parts, axis=0)).astype(BF16)
+    shape = (24, TAPS * LANES)
+    first = lax.broadcasted_iota(jnp.int32, shape, 0) % 8 * LANES
+    lane = lax.broadcasted_iota(jnp.int32, shape, 1)
+    chosen = jnp.where((lane >= first) & (lane < first + LANES), 1.0, 0.0).astype(BF16)
+    return jnp.dot(columns, chosen, preferred_element_type=F32)
 
 
 def inner_featured(signal, spread):
-    halves_total = [0.0, 0.0]
-    for offset in range(TAPS):
-        shifted = pltpu.roll(signal, offset, 1) if offset else signal
+    near, far = signal[:, :LANES], signal[:, LANES:]
+    lane = lane_numbers(near)
+    weight = spread[:, :LANES]
+    total_near, total_far = weight * near, weight * far
+    for offset in range(1, TAPS):
         weight = spread[:, offset * LANES : (offset + 1) * LANES]
-        for half in range(2):
-            part = weight * shifted[:, half * LANES : (half + 1) * LANES]
-            halves_total[half] = halves_total[half] + part if offset else part
-    return jnp.concatenate(halves_total, axis=1)
+        wrapped = jnp.where(lane >= LANES - offset, near, far)
+        total_near = total_near + weight * rolled(near, offset)
+        total_far = total_far + weight * rolled(wrapped, offset)
+    return jnp.concatenate([total_near, total_far], axis=1)
 
 
 def own_lanes(taps_ref, skip, group):
@@ -175,38 +188,19 @@
     return own
 
 
-def pack_kernel(
-    owners,
-    place_ref,
-    x_hbm,
-    cot_hbm,
-    filt_hbm,
-    w_hbm,
-    skip_hbm,
-    out_ref,
-    own_ref,
-    scratch,
-    x_ref,
-    cot_ref,
-    filt_ref,
-    w_ref,
-    skip_ref,
-    spread_ref,
-    sems,
-):
+def pack_kernel(owners, place_ref, *refs):
+    sources = refs[: 5 + TABLES]
+    out_ref, own_ref, feat_ref, spread_ref, wide_ref, cot_ref = refs[5 + TABLES : 11 + TABLES]
+    tables_here = refs[11 + TABLES : 11 + 2 * TABLES]
+    scratch, x_ref, filt_ref, w_ref, skip_ref, sems = refs[11 + 2 * TABLES :]
+    x_hbm, cot_hbm, filt_hbm, w_hbm, skip_hbm = sources[:5]
+    pairs = [(w_hbm, w_ref)]
+    pairs += [(x_hbm.at[stream], x_ref.at[stream]) for stream in (1, 2, 0)]
+    pairs += [(cot_hbm, cot_ref), (filt_hbm, filt_ref), (skip_hbm, skip_ref)]
+    pairs += list(zip(sources[5:], tables_here))
     copies = [
-        pltpu.make_async_copy(source, target, sems.at[place])
-        for place, (source, target) in enumerate(
-            [
-                (w_hbm, w_ref),
-                (x_hbm.at[1], x_ref.at[1]),
-                (x_hbm.at[2], x_ref.at[2]),
-                (x_hbm.at[0], x_ref.at[0]),
-                (cot_hbm, cot_ref),
-                (filt_hbm, filt_ref),
-                (skip_hbm, skip_ref),
-            ]
-        )
+        pltpu.make_async_copy(source, target, sems.at[number])
+        for number, (source, target) in enumerate(pairs)
     ]
     for copy in copies:
         copy.start()
@@ -216,7 +210,6 @@
     blank = jnp.zeros((pieces, LANES), F32)
     lane = lane_numbers(blank)
     rims = [blank, blank]
-    featured = {}
 
     def inner_part(value):
         return jnp.concatenate(
@@ -226,32 +219,34 @@
     copies[0].wait()
     for stream in range(3):
         spread_ref[stream] = spread_taps(w_ref[stream])
-    for place, stream in ((1, 1), (2, 2), (3, 0)):
-        copies[place].wait()
+    for number, stream in ((1, 1), (2, 2), (3, 0)):
+        copies[number].wait()
+        for start in range(0, 2 * pieces, CHUNK):
+            rows = slice(start, start + CHUNK)
+            signal = x_ref[stream, rows, :].astype(F32)
+            feat_ref[stream, rows, :] = inner_featured(signal, spread_ref[stream, rows, :])
         for side in range(2):
-            rows = slice(side * pieces, (side + 1) * pieces)
-            signal = x_ref[stream, rows, :].astype(F32)
-            featured[stream, side] = inner_featured(signal, spread_ref[stream, rows, :])
+            signal = x_ref[stream, side * pieces : (side + 1) * pieces, :].astype(F32)
+            ends = jnp.where(lane < RIM, signal[:, :LANES], signal[:, LANES:])
             first = 2 * RIM * (stream * 2 + side)
-            rims[side] = put_lanes(rims[side], first, RIM, signal[:, LANES:], LANES - RIM)
-            rims[side] = put_lanes(rims[side], first + RIM, RIM, signal[:, :LANES])
-    products, mixed = [], []
+            rims[side] = put_lanes(rims[side], first, 2 * RIM, ends, LANES - RIM)
+    tops = []
     for side in range(2):
-        products.append(inner_part(featured[1, side] * featured[2, side]))
+        rows = slice(side * pieces, (side + 1) * pieces)
+        product = inner_part(feat_ref[1, rows, :] * feat_ref[2, rows, :])
+        code, top = encoded(exchanged(product, member, owners))
+        lines.put_block(IN_PROD + 2 * side, code)
+        tops.append(top)
     copies[4].wait()
     for side in range(2):
-        cot = cot_ref[side * pieces : (side + 1) * pieces, :]
-        mixed.append(inner_part(featured[0, side] * cot))
+        rows = slice(side * pieces, (side + 1) * pieces)
+        cot = cot_ref[rows, :]
+        code, top = encoded(exchanged(inner_part(feat_ref[0, rows, :] * cot), member, owners))
+        lines.put_block(IN_MIXED + 2 * side, code)
+        tops.append(top)
         high = cot[:, :LANES].astype(BF16).astype(F32)
-        first = COT_LANE + 2 * RIM * side
-        rims[side] = put_lanes(rims[side], first, RIM, high)
-        rims[side] = put_lanes(rims[side], first + RIM, RIM, cot[:, :LANES] - high)
-    tops = []
-    for row, values in ((IN_PROD, products), (IN_MIXED, mixed)):
-        for side in range(2):
-            code, top = encoded(exchanged(values[side], member, owners))
-            lines.put_block(row + 2 * side, code)
-            tops.append(top)
+        both = jnp.where(lane < RIM, high, rolled(cot[:, :LANES] - high, RIM))
+        rims[side] = put_lanes(rims[side], COT_LANE + 2 * RIM * side, 2 * RIM, both)
     copies[5].wait()
     code, top = encoded(filt_ref[...])
     lines.put_block(IN_FILT, jnp.concatenate([code] * owners, axis=0))
@@ -262,6 +257,10 @@
     out_ref[...] = scratch[...].astype(BF16)
     copies[6].wait()
     own_ref[...] = own_lanes(w_ref, skip_ref[...], place_ref[1])
+    column = jnp.transpose(jnp.broadcast_to(skip_ref[...], (8, LANES)))[:, 0:1]
+    wide_ref[...] = jnp.broadcast_to(column, wide_ref.shape)
+    for copy in copies[7:]:
+        copy.wait()
 
 
 def turned(re, im, twiddle):
@@ -444,31 +443,6 @@
     out_ref[...] = scratch[...].astype(BF16)
 
 
-def feature_kernel(*refs):
-    x_hbm, w_hbm, skip_hbm = refs[:3]
-    out_ref, spread_ref, wide_ref = refs[3 + TABLES : 6 + TABLES]
-    x_ref, w_ref, skip_ref, sems = refs[6 + 2 * TABLES :]
-    pairs = [(w_hbm, w_ref), (x_hbm, x_ref), (skip_hbm, skip_ref)]
-    pairs += list(zip(refs[3 : 3 + TABLES], refs[6 + TABLES : 6 + 2 * TABLES]))
-    copies = [
-        pltpu.make_async_copy(source, target, sems.at[place])
-        for place, (source, target) in enumerate(pairs)
-    ]
-    for copy in copies:
-        copy.start()
-    copies[0].wait()
-    for stream in range(3):
-        spread_ref[stream] = spread_taps(w_ref[stream])
-    copies[1].wait()
-    for stream in range(3):
-        out_ref[stream] = inner_featured(x_ref[stream].astype(F32), spread_ref[stream])
-    copies[2].wait()
-    column = jnp.transpose(jnp.broadcast_to(skip_ref[...], (8, LANES)))[:, 0:1]
-    wide_ref[...] = jnp.broadcast_to(column, wide_ref.shape)
-    for copy in copies[3:]:
-        copy.wait()
-
-
 def local_kernel(
     owners,
     r_ref,
@@ -510,36 +484,6 @@
     def first_lanes(array, place):
         return rolled(array, -2 * RIM * place)
 
-    for side in range(2):
-        rows = slice(side * pieces, (side + 1) * pieces)
-        featured = []
-        for stream in range(3):
-            inside = feat_ref[stream, rows, :]
-            left = first_lanes(head, stream * 2 + side)
-            left = jnp.where(lane < RIM, left, inside[:, :LANES])
-            featured.append(jnp.concatenate([left, inside[:, LANES:]], axis=1))
-        query, key, value = featured
-        cot = cot_ref[rows, :]
-        skip = jnp.concatenate([skip_ref[rows, :]] * 2, axis=1)
-        long_out = exchanged(block(OUT_LONG + 2 * side, side), member, owners)
-        mixer = long_out + skip * (key * value)
-        out_room[rows, :] = query * mixer
-        send(out_room.at[rows, :], out_ref.at[rows, :])
-        grad_long = exchanged(block(OUT_GRAD + 2 * side, 2 + side), member, owners)
-        grad_product = grad_long + skip * (cot * query)
-        for stream, grad in enumerate((cot * mixer, grad_product * value, grad_product * key)):
-            after = first_lanes(rim, stream * 2 + side)
-            near, far = grad[:, :LANES], grad[:, LANES:]
-            weight = w_ref[stream, rows, :LANES]
-            total_near, total_far = weight * near, weight * far
-            for offset in range(1, TAPS):
-                weight = w_ref[stream, rows, offset * LANES : (offset + 1) * LANES]
-                wrapped = lane < offset
-                total_near = total_near + weight * rolled(jnp.where(wrapped, far, near), -offset)
-                total_far = total_far + weight * rolled(jnp.where(wrapped, after, far), -offset)
-            grad_room[stream, rows, :LANES] = total_near
-            grad_room[stream, rows, LANES:] = total_far
-            send(grad_room.at[stream, rows, :], grad_ref.at[stream, rows, :])
     partial = block(OUT_FILT, 4)
     owned = pieces // owners
     total = partial[:owned]
@@ -547,6 +491,44 @@
         total = total + partial[place * owned : (place + 1) * owned]
     tail_room[...] = total
     send(tail_room, tail_ref)
+    lane = lane[:CHUNK]
+    for side in range(2):
+        long_out = exchanged(block(OUT_LONG + 2 * side, side), member, owners)
+        grad_long = exchanged(block(OUT_GRAD + 2 * side, 2 + side), member, owners)
+        lefts = [first_lanes(head, stream * 2 + side) for stream in range(3)]
+        afters = [first_lanes(rim, stream * 2 + side) for stream in range(3)]
+        for start in range(0, pieces, CHUNK):
+            part = slice(start, start + CHUNK)
+            rows = slice(side * pieces + start, side * pieces + start + CHUNK)
+            featured = []
+            for stream in range(3):
+                inside = feat_ref[stream, rows, :]
+                left = jnp.where(lane < RIM, lefts[stream][part], inside[:, :LANES])
+                featured.append(jnp.concatenate([left, inside[:, LANES:]], axis=1))
+            query, key, value = featured
+            cot = cot_ref[rows, :]
+            skip = jnp.concatenate([skip_ref[rows, :]] * 2, axis=1)
+            mixer = long_out[part] + skip * (key * value)
+            out_room[rows, :] = query * mixer
+            grad_product = grad_long[part] + skip * (cot * query)
+            for stream, grad in enumerate((cot * mixer, grad_product * value, grad_product * key)):
+                after = afters[stream][part]
+                near, far = grad[:, :LANES], grad[:, LANES:]
+                weight = w_ref[stream, rows, :LANES]
+                total_near, total_far = weight * near, weight * far
+                for offset in range(1, TAPS):
+                    weight = w_ref[stream, rows, offset * LANES : (offset + 1) * LANES]
+                    wrapped = lane < offset
+                    moved = rolled(jnp.where(wrapped, far, near), -offset)
+                    total_near = total_near + weight * moved
+                    moved = rolled(jnp.where(wrapped, after, far), -offset)
+                    total_far = total_far + weight * moved
+                grad_room[stream, rows, :LANES] = total_near
+                grad_room[stream, rows, LANES:] = total_far
+        rows = slice(side * pieces, (side + 1) * pieces)
+        send(out_room.at[rows, :], out_ref.at[rows, :])
+        for stream in range(3):
+            send(grad_room.at[stream, rows, :], grad_ref.at[stream, rows, :])
     for copy in copies:
         copy.wait()
 
@@ -585,9 +567,6 @@
     def shape(*dims, dtype=F32):
         return jax.ShapeDtypeStruct(dims, dtype)
 
-    def pinned(array):
-        return pltpu.with_memory_space_constraint(array, pltpu.HBM)
-
     def room(rows):
         return pltpu.VMEM((pieces * rows, LANES), F32)
 
@@ -600,42 +579,31 @@
     place = jnp.stack([member, group]).astype(jnp.int32)
     taps = jnp.transpose(short_weight, (0, 2, 1))
     skip_row = skip[None]
-    sent, own = call(
+    constants = [jnp.asarray(table) for table in tables(pieces, length, scale)]
+    arguments = (inputs, cotangent, filters, taps, skip_row, *constants)
+    sent, own, featured, spread, skip_wide, cot, *constants = call(
         functools.partial(pack_kernel, owners),
-        (shape(pieces * IN_ROWS, LANES, dtype=BF16), shape(8, LANES)),
-        (place, *(pinned(array) for array in (inputs, cotangent, filters, taps, skip_row))),
+        (
+            shape(pieces * IN_ROWS, LANES, dtype=BF16),
+            shape(8, LANES),
+            shape(3, channels, length),
+            shape(3, channels, TAPS * LANES),
+            shape(channels, LANES),
+            shape(channels, length),
+            *(shape(*table.shape, dtype=table.dtype) for table in constants),
+        ),
+        (place, *(pltpu.with_memory_space_constraint(array, pltpu.HBM) for array in arguments)),
         [
             room(IN_ROWS),
             pltpu.VMEM(inputs.shape, BF16),
-            pltpu.VMEM(cotangent.shape, F32),
             pltpu.VMEM(filters.shape, F32),
             pltpu.VMEM(taps.shape, F32),
             pltpu.VMEM(skip_row.shape, F32),
-            pltpu.VMEM((3, channels, TAPS * LANES), F32),
-            pltpu.SemaphoreType.DMA((7,)),
+            pltpu.SemaphoreType.DMA((7 + TABLES,)),
         ],
-        specs={0: SMEM_SPEC, **{operand: HBM_SPEC for operand in range(1, 6)}},
+        specs={0: SMEM_SPEC, **{operand: HBM_SPEC for operand in range(1, 6 + TABLES)}},
     )
     received = transposed(sent)
-    constants = [jnp.asarray(table) for table in tables(pieces, length, scale)]
-    beside = call(
-        feature_kernel,
-        (
-            shape(3, channels, length),
-            shape(3, channels, TAPS * LANES),
-            shape(channels, LANES),
-            *(shape(*table.shape, dtype=table.dtype) for table in constants),
-        ),
-        [pinned(array) for array in (inputs, taps, skip_row, *constants)],
-        [
-            *(pltpu.VMEM(array.shape, array.dtype) for array in (inputs, taps, skip_row)),
-            pltpu.SemaphoreType.DMA((3 + TABLES,)),
-        ],
-        specs={operand: HBM_SPEC for operand in range(3 + TABLES)},
-        flops=10000000,
-    )
-    received, beside = lax.optimization_barrier((received, beside))
-    beside, constants = beside[:3], beside[3:]
     cross, spectra, kept = call(
         forward_kernel,
         (
@@ -665,7 +633,7 @@
     return call(
         functools.partial(local_kernel, owners),
         (shape(channels, length), shape(3, channels, length), shape(owned, length)),
-        (received, place, *beside, cotangent),
+        (received, place, featured, spread, skip_wide, cot),
         [
             room(OUT_ROWS),
             pltpu.VMEM((channels, length), F32),

time: 65.5 us -> 64 us (0.977)
  blocking collectives: 24.9 us -> 53.7 us
  starting transfers between devices: 17.8 us -> 0.67 us
  waiting for transfers between devices: 9.75 us -> 0.01 us
  Pallas kernels: 11.5 us -> 8.21 us
    all_to_all x1 -> x2, blocking collectives: 24.9 us -> 53.7 us  [transposed(): lax.all_to_all(array.reshape(pieces, rows // 2, 2, LANES), 'ctx', 0, 0)]
    all_to_all x1 -> x0, starting transfers between devices: 17.1 us -> none  [transposed(): lax.all_to_all(array.reshape(pieces, rows // 2, 2, LANES), 'ctx', 0, 0)]
    all_to_all x1 -> x0, waiting for transfers between devices: 9.74 us -> none  [transposed(): lax.all_to_all(array.reshape(pieces, rows // 2, 2, LANES), 'ctx', 0, 0)]
    pallas_call x5 -> x4, Pallas kernels: 11.5 us -> 8.21 us  [call(): pl.pallas_call(kernel, out_shape=out_shape, in_specs=[specs.get(place, VM...]
  transfers between devices with their start and end apart: 2 -> 1, of which waited for: 1 -> 0; matrix products, arithmetic and copies ran while one was open for 0% -> 0% of each run, Pallas kernels for 3% -> 0%
where the time goes in v3:
time: 64 us; the launch traced here: 63.3 us
  blocking collectives  53.7 us (84%)
  Pallas kernels  8.21 us (13%)
  between operations  0.69 us (1%)
  starting transfers between devices  0.67 us (1%)
    all_to_all x2, blocking collectives, transposed(): lax.all_to_all(array.reshape(pieces, rows // 2, 2, LANES), 'ctx', 0, 0)  53.7 us
    pallas_call x4, Pallas kernels, call(): pl.pallas_call(kernel, out_shape=out_shape, in_specs=[specs.get(place, VM...  8.21 us
  transfers between devices with their start and end apart: 1, of which 0 were waited for; matrix products, arithmetic and copies ran while one was open for 0% of the time, Pallas kernels for 0%

profile of v3, /device:TPU:1, one launch (start us, length us, event | category | flops | bytes accessed | tf_op | source)
XLA Modules:
  0.0 63.3 jit_solution(10062459040107115659)
XLA Ops:
  0.7 0.1 pad_add_fusion.place_ref
  0.7 3.0 %shard_map.139 = (bf16[768,128]{1,0:T(8,128)(2,1)S(1)}, f32[8,128]{1,0:T(8,128)S(1)}, f32[3,128,256]{2,1,0:T(8,128)S(1)}, f32[3,128,896]{2,1,0:T(8,128)S(1)}, f3...) custom-call(s32[2]{0:T(128)S(1)} %pad_add_fusion.place_ref, ...), custom_call_target="tpu_custom_call" | custom-call | bytes 1048576 | tf_op jit(solution)/shard_map/pallas_call | solution.py:546
  3.7 28.8 %all_to_all.10 = bf16[64,6,2,128]{3,2,1,0:T(2,128)(2,1)S(1)} all-to-all(bf16[64,6,2,128]{3,2,1,0:T(2,128)(2,1)S(1)} %bitcast.9), channel_id=1, replica_groups=mesh['ctx'=64,'ch'=8] {'ctx'}, dimensions={0} | all-to-all | bytes 393216 | tf_op jit(solution)/shard_map/all_to_all | solution.py:575
  32.5 1.5 %shard_map.140 = (bf16[320,128]{1,0:T(8,128)(2,1)S(1)}, f32[512,256]{1,0:T(8,128)S(1)}, f32[6,64,128]{2,1,0:T(8,128)S(1)}) custom-call(bf16[768,128]{1,0:T(8,128)(2,1)S(1)} %bitcast.11, f32[8,128]{1,0:T(8,128)S(1)} %get-tuple-element.20.w_ref, bf16[256,128]{1,0:T(8,128)(2,1)S(1)} %get-tuple-element.21.outer_hi, ...), custom_call_target="tpu_custom_call" | custom-call | flops 800000000 | bytes 1048576 | tf_op jit(solution)/shard_map/pallas_call | solution.py:546
  34.0 0.7 %collective-permute-start = (bf16[320,128]{1,0:T(8,128)(2,1)S(1)}, bf16[320,128]{1,0:T(8,128)(2,1)S(1)}, u32[]{:S(2)}, u32[]{:S(2)}) collective-permute-start(bf16[320,128]{1,0:T(8,128)(2,1)S(1)} %get-tuple-element.28), channel_id=1, source_target_pairs={{0,0},{1,1},{2,2},{3,3},{4,4},{5,5},{6,6},{7,7},{8,8},{9,9},{10,10... | collective-permute-start | bytes 245768 | tf_op jit(solution)/shard_map/ppermute | solution.py:623
  34.7 0.0 collective-permute-done.cross_ref
  34.7 1.4 %shard_map.141 = bf16[768,128]{1,0:T(8,128)(2,1)S(1)} custom-call(bf16[320,128]{1,0:T(8,128)(2,1)S(1)} %collective-permute-done.cross_ref, f32[512,256]{1,0:T(8,128)S(1)} %get-tuple-element.29.spec_ref, f32[6,64,128]{2,1,0:T(8,128)S(1)} %get-tuple-element.30.kept_ref, f32[8,128]{1,0:T(8,128)S(1)} %get-tuple-element.20.w_ref, ...), custom_call_target="tpu_custom_call" | custom-call | flops 800000000 | bytes 1048576 | tf_op jit(solution)/shard_map/pallas_call | solution.py:546
  36.1 24.9 %all_to_all.11 = bf16[64,6,2,128]{3,2,1,0:T(2,128)(2,1)S(1)} all-to-all(bf16[64,6,2,128]{3,2,1,0:T(2,128)(2,1)S(1)} %bitcast.10), channel_id=1, replica_groups=mesh['ctx'=64,'ch'=8] {'ctx'}, dimensions={0} | all-to-all | bytes 393216 | tf_op jit(solution)/shard_map/all_to_all | solution.py:575
  61.0 2.3 %shard_map.142 = (f32[128,256]{1,0:T(8,128)}, f32[3,128,256]{2,1,0:T(8,128)}, f32[8,256]{1,0:T(8,128)}) custom-call(bf16[768,128]{1,0:T(8,128)(2,1)S(1)} %bitcast.8, s32[2]{0:T(128)S(1)} %pad_add_fusion.place_ref, f32[3,128,256]{2,1,0:T(8,128)S(1)} %get-tuple-element.31.feat_ref, f32[3,128,896]{2,1,0:T(8,128)S(1)} %get-tuple-element.32.w_ref, ...), custom_call_target="tpu_custom_call" | custom-call | bytes 1048576 | tf_op jit(solution)/shard_map/pallas_call | solution.py:546
Async XLA Ops:
  34.0 0.7 %collective-permute-start = (bf16[320,128]{1,0:T(8,128)(2,1)S(1)}, bf16[320,128]{1,0:T(8,128)(2,1)S(1)}, u32[]{:S(2)}, u32[]{:S(2)}) collective-permute-start(bf16[320,128]{1,0:T(8,128)(2,1)S(1)} %get-tuple-element.28), channel_id=1, source_target_pairs={{0,0},{1,1},{2,2},{3,3},{4,4},{5,5},{6,6},{7,7},{8,8},{9,9},{10,10... | collective-permute-start | bytes 245768 | tf_op jit(solution)/shard_map/ppermute | solution.py:623

commit v4 on v3

--- a/solution.py
+++ b/solution.py
@@ -188,7 +188,7 @@
     return own
 
 
-def pack_kernel(owners, place_ref, *refs):
+def pack_kernel(owners, *refs):
     sources = refs[: 5 + TABLES]
     out_ref, own_ref, feat_ref, spread_ref, wide_ref, cot_ref = refs[5 + TABLES : 11 + TABLES]
     tables_here = refs[11 + TABLES : 11 + 2 * TABLES]
@@ -206,7 +206,10 @@
         copy.start()
     lines = Lines(scratch, IN_ROWS)
     pieces = lines.count
-    member = place_ref[0]
+    member = lax.axis_index("ch")
+    position = lax.axis_index("ctx")
+    owned = pieces // owners
+    group = ((position // owned) ^ member) * owned + position % owned
     blank = jnp.zeros((pieces, LANES), F32)
     lane = lane_numbers(blank)
     rims = [blank, blank]
@@ -256,7 +259,7 @@
     lines.put(IN_RIM + 1, blank)
     out_ref[...] = scratch[...].astype(BF16)
     copies[6].wait()
-    own_ref[...] = own_lanes(w_ref, skip_ref[...], place_ref[1])
+    own_ref[...] = own_lanes(w_ref, skip_ref[...], group)
     column = jnp.transpose(jnp.broadcast_to(skip_ref[...], (8, LANES)))[:, 0:1]
     wide_ref[...] = jnp.broadcast_to(column, wide_ref.shape)
     for copy in copies[7:]:
@@ -446,7 +449,6 @@
 def local_kernel(
     owners,
     r_ref,
-    place_ref,
     feat_ref,
     w_ref,
     skip_ref,
@@ -460,7 +462,7 @@
     tail_room,
     sems,
 ):
-    member = place_ref[0]
+    member = lax.axis_index("ch")
     scratch[...] = r_ref[...].astype(F32)
     lines = Lines(scratch, OUT_ROWS)
     pieces = lines.count
@@ -534,7 +536,6 @@
 
 
 VMEM_SPEC = pl.BlockSpec(memory_space=pltpu.VMEM)
-SMEM_SPEC = pl.BlockSpec(memory_space=pltpu.SMEM)
 ANY_SPEC = pl.BlockSpec(memory_space=pl.ANY)
 HBM_SPEC = pl.BlockSpec(memory_space=pltpu.HBM)
 
@@ -557,8 +558,6 @@
 def shards(inputs, short_weight, skip, filters, cotangent):
     pieces = lax.axis_size("ctx")
     owners = lax.axis_size("ch")
-    position = lax.axis_index("ctx")
-    member = lax.axis_index("ch")
     _, channels, length = inputs.shape
     owned = filters.shape[0]
     count = 2 * pieces
@@ -575,8 +574,6 @@
         array = lax.all_to_all(array.reshape(pieces, rows // 2, 2, LANES), "ctx", 0, 0)
         return array.reshape(pieces * rows, LANES)
 
-    group = ((position // owned) ^ member) * owned + position % owned
-    place = jnp.stack([member, group]).astype(jnp.int32)
     taps = jnp.transpose(short_weight, (0, 2, 1))
     skip_row = skip[None]
     constants = [jnp.asarray(table) for table in tables(pieces, length, scale)]
@@ -592,7 +589,7 @@
             shape(channels, length),
             *(shape(*table.shape, dtype=table.dtype) for table in constants),
         ),
-        (place, *(pltpu.with_memory_space_constraint(array, pltpu.HBM) for array in arguments)),
+        [pltpu.with_memory_space_constraint(array, pltpu.HBM) for array in arguments],
         [
             room(IN_ROWS),
             pltpu.VMEM(inputs.shape, BF16),
@@ -601,7 +598,7 @@
             pltpu.VMEM(skip_row.shape, F32),
             pltpu.SemaphoreType.DMA((7 + TABLES,)),
         ],
-        specs={0: SMEM_SPEC, **{operand: HBM_SPEC for operand in range(1, 6 + TABLES)}},
+        specs={operand: HBM_SPEC for operand in range(5 + TABLES)},
     )
     received = transposed(sent)
     cross, spectra, kept = call(
@@ -633,7 +630,7 @@
     return call(
         functools.partial(local_kernel, owners),
         (shape(channels, length), shape(3, channels, length), shape(owned, length)),
-        (received, place, featured, spread, skip_wide, cot),
+        (received, featured, spread, skip_wide, cot),
         [
             room(OUT_ROWS),
             pltpu.VMEM((channels, length), F32),
@@ -641,7 +638,6 @@
             pltpu.VMEM((owned, length), F32),
             pltpu.SemaphoreType.DMA((9,)),
         ],
-        specs={1: SMEM_SPEC},
         out_spec=ANY_SPEC,
     )
 

time: 64 us -> 62.8 us (0.981)
  Pallas kernels: 8.21 us -> 7.08 us
    pallas_call x4, Pallas kernels: 8.21 us -> 7.08 us  [call(): pl.pallas_call(kernel, out_shape=out_shape, in_specs=[specs.get(place, VM...]
where the time goes in v4:
time: 62.8 us; the launch traced here: 62.1 us
  blocking collectives  53.7 us (86%)
  Pallas kernels  7.08 us (11%)
  starting transfers between devices  0.67 us (1%)
  between operations  0.67 us (1%)
    all_to_all x2, blocking collectives, transposed(): lax.all_to_all(array.reshape(pieces, rows // 2, 2, LANES), 'ctx', 0, 0)  53.7 us
    pallas_call x4, Pallas kernels, call(): pl.pallas_call(kernel, out_shape=out_shape, in_specs=[specs.get(place, VM...  7.08 us
  transfers between devices with their start and end apart: 1, of which 0 were waited for; matrix products, arithmetic and copies ran while one was open for 0% of the time, Pallas kernels for 0%

profile of v4, /device:TPU:1, one launch (start us, length us, event | category | flops | bytes accessed | tf_op | source)
XLA Modules:
  0.0 62.1 jit_solution(2772190252087074704)
XLA Ops:
  0.6 2.4 %shard_map.139 = (bf16[768,128]{1,0:T(8,128)(2,1)S(1)}, f32[8,128]{1,0:T(8,128)S(1)}, f32[3,128,256]{2,1,0:T(8,128)S(1)}, f32[3,128,896]{2,1,0:T(8,128)S(1)}, f3...) custom-call(bf16[3,128,256]{2,1,0:T(8,128)(2,1)} %refs_0_.1, ...), custom_call_target="tpu_custom_call" | custom-call | bytes 1048576 | tf_op jit(solution)/shard_map/pallas_call | solution.py:547
  3.1 28.8 %all_to_all.10 = bf16[64,6,2,128]{3,2,1,0:T(2,128)(2,1)S(1)} all-to-all(bf16[64,6,2,128]{3,2,1,0:T(2,128)(2,1)S(1)} %bitcast.7), channel_id=1, replica_groups=mesh['ctx'=64,'ch'=8] {'ctx'}, dimensions={0} | all-to-all | bytes 393216 | tf_op jit(solution)/shard_map/all_to_all | solution.py:574
  31.9 1.5 %shard_map.140 = (bf16[320,128]{1,0:T(8,128)(2,1)S(1)}, f32[512,256]{1,0:T(8,128)S(1)}, f32[6,64,128]{2,1,0:T(8,128)S(1)}) custom-call(bf16[768,128]{1,0:T(8,128)(2,1)S(1)} %bitcast.9, f32[8,128]{1,0:T(8,128)S(1)} %get-tuple-element.20.w_ref, bf16[256,128]{1,0:T(8,128)(2,1)S(1)} %get-tuple-element.21.outer_hi, ...), custom_call_target="tpu_custom_call" | custom-call | flops 800000000 | bytes 1048576 | tf_op jit(solution)/shard_map/pallas_call | solution.py:547
  33.3 0.7 %collective-permute-start = (bf16[320,128]{1,0:T(8,128)(2,1)S(1)}, bf16[320,128]{1,0:T(8,128)(2,1)S(1)}, u32[]{:S(2)}, u32[]{:S(2)}) collective-permute-start(bf16[320,128]{1,0:T(8,128)(2,1)S(1)} %get-tuple-element.28), channel_id=1, source_target_pairs={{0,0},{1,1},{2,2},{3,3},{4,4},{5,5},{6,6},{7,7},{8,8},{9,9},{10,10... | collective-permute-start | bytes 245768 | tf_op jit(solution)/shard_map/ppermute | solution.py:620
  34.0 0.0 collective-permute-done.cross_ref
  34.0 1.4 %shard_map.141 = bf16[768,128]{1,0:T(8,128)(2,1)S(1)} custom-call(bf16[320,128]{1,0:T(8,128)(2,1)S(1)} %collective-permute-done.cross_ref, f32[512,256]{1,0:T(8,128)S(1)} %get-tuple-element.29.spec_ref, f32[6,64,128]{2,1,0:T(8,128)S(1)} %get-tuple-element.30.kept_ref, f32[8,128]{1,0:T(8,128)S(1)} %get-tuple-element.20.w_ref, ...), custom_call_target="tpu_custom_call" | custom-call | flops 800000000 | bytes 1048576 | tf_op jit(solution)/shard_map/pallas_call | solution.py:547
  35.4 24.9 %all_to_all.11 = bf16[64,6,2,128]{3,2,1,0:T(2,128)(2,1)S(1)} all-to-all(bf16[64,6,2,128]{3,2,1,0:T(2,128)(2,1)S(1)} %bitcast.8), channel_id=1, replica_groups=mesh['ctx'=64,'ch'=8] {'ctx'}, dimensions={0} | all-to-all | bytes 393216 | tf_op jit(solution)/shard_map/all_to_all | solution.py:574
  60.4 1.8 %shard_map.142 = (f32[128,256]{1,0:T(8,128)}, f32[3,128,256]{2,1,0:T(8,128)}, f32[8,256]{1,0:T(8,128)}) custom-call(bf16[768,128]{1,0:T(8,128)(2,1)S(1)} %bitcast.6, f32[3,128,256]{2,1,0:T(8,128)S(1)} %get-tuple-element.31.feat_ref, f32[3,128,896]{2,1,0:T(8,128)S(1)} %get-tuple-element.32.w_ref, f32[128,128]{1,0:T(8,128)S(1)} %get-tuple-element.33.skip_ref, ...), custom_call_target="tpu_custom_call" | custom-call | bytes 1048576 | tf_op jit(solution)/shard_map/pallas_call | solution.py:547
Async XLA Ops:
  33.3 0.7 %collective-permute-start = (bf16[320,128]{1,0:T(8,128)(2,1)S(1)}, bf16[320,128]{1,0:T(8,128)(2,1)S(1)}, u32[]{:S(2)}, u32[]{:S(2)}) collective-permute-start(bf16[320,128]{1,0:T(8,128)(2,1)S(1)} %get-tuple-element.28), channel_id=1, source_target_pairs={{0,0},{1,1},{2,2},{3,3},{4,4},{5,5},{6,6},{7,7},{8,8},{9,9},{10,10... | collective-permute-start | bytes 245768 | tf_op jit(solution)/shard_map/ppermute | solution.py:620

commit v5 on v4

--- a/solution.py
+++ b/solution.py
@@ -194,9 +194,9 @@
     tables_here = refs[11 + TABLES : 11 + 2 * TABLES]
     scratch, x_ref, filt_ref, w_ref, skip_ref, sems = refs[11 + 2 * TABLES :]
     x_hbm, cot_hbm, filt_hbm, w_hbm, skip_hbm = sources[:5]
-    pairs = [(w_hbm, w_ref)]
+    pairs = [(w_hbm, w_ref), (filt_hbm, filt_ref), (skip_hbm, skip_ref)]
     pairs += [(x_hbm.at[stream], x_ref.at[stream]) for stream in (1, 2, 0)]
-    pairs += [(cot_hbm, cot_ref), (filt_hbm, filt_ref), (skip_hbm, skip_ref)]
+    pairs += [(cot_hbm, cot_ref)]
     pairs += list(zip(sources[5:], tables_here))
     copies = [
         pltpu.make_async_copy(source, target, sems.at[number])
@@ -222,8 +222,15 @@
     copies[0].wait()
     for stream in range(3):
         spread_ref[stream] = spread_taps(w_ref[stream])
-    for number, stream in ((1, 1), (2, 2), (3, 0)):
-        copies[number].wait()
+    for copy in copies[1:7]:
+        copy.wait()
+    code, filt_top = encoded(filt_ref[...])
+    lines.put_block(IN_FILT, jnp.concatenate([code] * owners, axis=0))
+    lines.put(IN_RIM + 1, blank)
+    own_ref[...] = own_lanes(w_ref, skip_ref[...], group)
+    column = jnp.transpose(jnp.broadcast_to(skip_ref[...], (8, LANES)))[:, 0:1]
+    wide_ref[...] = jnp.broadcast_to(column, wide_ref.shape)
+    for stream in (1, 2, 0):
         for start in range(0, 2 * pieces, CHUNK):
             rows = slice(start, start + CHUNK)
             signal = x_ref[stream, rows, :].astype(F32)
@@ -240,7 +247,6 @@
         code, top = encoded(exchanged(product, member, owners))
         lines.put_block(IN_PROD + 2 * side, code)
         tops.append(top)
-    copies[4].wait()
     for side in range(2):
         rows = slice(side * pieces, (side + 1) * pieces)
         cot = cot_ref[rows, :]
@@ -250,18 +256,10 @@
         high = cot[:, :LANES].astype(BF16).astype(F32)
         both = jnp.where(lane < RIM, high, rolled(cot[:, :LANES] - high, RIM))
         rims[side] = put_lanes(rims[side], COT_LANE + 2 * RIM * side, 2 * RIM, both)
-    copies[5].wait()
-    code, top = encoded(filt_ref[...])
-    lines.put_block(IN_FILT, jnp.concatenate([code] * owners, axis=0))
-    tops.append(jnp.concatenate([top] * owners, axis=0))
+    tops.append(jnp.concatenate([filt_top] * owners, axis=0))
     rim = exchanged(rims[0] + rims[1], member, owners)
     lines.put(IN_RIM, in_lanes(tops, IN_TOP_LANE, rim))
-    lines.put(IN_RIM + 1, blank)
     out_ref[...] = scratch[...].astype(BF16)
-    copies[6].wait()
-    own_ref[...] = own_lanes(w_ref, skip_ref[...], group)
-    column = jnp.transpose(jnp.broadcast_to(skip_ref[...], (8, LANES)))[:, 0:1]
-    wide_ref[...] = jnp.broadcast_to(column, wide_ref.shape)
     for copy in copies[7:]:
         copy.wait()
 

time: 62.8 us -> 62.3 us (level)
  no operation moved by 1% of the time
where the time goes in v5:
time: 62.3 us; the launch traced here: 61.7 us
  blocking collectives  53.7 us (86%)
  Pallas kernels  6.68 us (11%)
  starting transfers between devices  0.67 us (1%)
  between operations  0.67 us (1%)
    all_to_all x2, blocking collectives, transposed(): lax.all_to_all(array.reshape(pieces, rows // 2, 2, LANES), 'ctx', 0, 0)  53.7 us
    pallas_call x4, Pallas kernels, call(): pl.pallas_call(kernel, out_shape=out_shape, in_specs=[specs.get(place, VM...  6.68 us
  transfers between devices with their start and end apart: 1, of which 0 were waited for; matrix products, arithmetic and copies ran while one was open for 0% of the time, Pallas kernels for 0%

profile of v5, /device:TPU:1, one launch (start us, length us, event | category | flops | bytes accessed | tf_op | source)
XLA Modules:
  0.0 61.7 jit_solution(15220716381571932275)
XLA Ops:
  0.6 2.0 %shard_map.139 = (bf16[768,128]{1,0:T(8,128)(2,1)S(1)}, f32[8,128]{1,0:T(8,128)S(1)}, f32[3,128,256]{2,1,0:T(8,128)S(1)}, f32[3,128,896]{2,1,0:T(8,128)S(1)}, f3...) custom-call(bf16[3,128,256]{2,1,0:T(8,128)(2,1)} %refs_0_.1, ...), custom_call_target="tpu_custom_call" | custom-call | bytes 1048576 | tf_op jit(solution)/shard_map/pallas_call | solution.py:545
  2.7 28.8 %all_to_all.10 = bf16[64,6,2,128]{3,2,1,0:T(2,128)(2,1)S(1)} all-to-all(bf16[64,6,2,128]{3,2,1,0:T(2,128)(2,1)S(1)} %bitcast.7), channel_id=1, replica_groups=mesh['ctx'=64,'ch'=8] {'ctx'}, dimensions={0} | all-to-all | bytes 393216 | tf_op jit(solution)/shard_map/all_to_all | solution.py:572
  31.5 1.5 %shard_map.140 = (bf16[320,128]{1,0:T(8,128)(2,1)S(1)}, f32[512,256]{1,0:T(8,128)S(1)}, f32[6,64,128]{2,1,0:T(8,128)S(1)}) custom-call(bf16[768,128]{1,0:T(8,128)(2,1)S(1)} %bitcast.9, f32[8,128]{1,0:T(8,128)S(1)} %get-tuple-element.20.w_ref, bf16[256,128]{1,0:T(8,128)(2,1)S(1)} %get-tuple-element.21.outer_hi, ...), custom_call_target="tpu_custom_call" | custom-call | flops 800000000 | bytes 1048576 | tf_op jit(solution)/shard_map/pallas_call | solution.py:545
  32.9 0.7 %collective-permute-start = (bf16[320,128]{1,0:T(8,128)(2,1)S(1)}, bf16[320,128]{1,0:T(8,128)(2,1)S(1)}, u32[]{:S(2)}, u32[]{:S(2)}) collective-permute-start(bf16[320,128]{1,0:T(8,128)(2,1)S(1)} %get-tuple-element.28), channel_id=1, source_target_pairs={{0,0},{1,1},{2,2},{3,3},{4,4},{5,5},{6,6},{7,7},{8,8},{9,9},{10,10... | collective-permute-start | bytes 245768 | tf_op jit(solution)/shard_map/ppermute | solution.py:618
  33.6 0.0 collective-permute-done.cross_ref
  33.6 1.4 %shard_map.141 = bf16[768,128]{1,0:T(8,128)(2,1)S(1)} custom-call(bf16[320,128]{1,0:T(8,128)(2,1)S(1)} %collective-permute-done.cross_ref, f32[512,256]{1,0:T(8,128)S(1)} %get-tuple-element.29.spec_ref, f32[6,64,128]{2,1,0:T(8,128)S(1)} %get-tuple-element.30.kept_ref, f32[8,128]{1,0:T(8,128)S(1)} %get-tuple-element.20.w_ref, ...), custom_call_target="tpu_custom_call" | custom-call | flops 800000000 | bytes 1048576 | tf_op jit(solution)/shard_map/pallas_call | solution.py:545
  35.0 24.9 %all_to_all.11 = bf16[64,6,2,128]{3,2,1,0:T(2,128)(2,1)S(1)} all-to-all(bf16[64,6,2,128]{3,2,1,0:T(2,128)(2,1)S(1)} %bitcast.8), channel_id=1, replica_groups=mesh['ctx'=64,'ch'=8] {'ctx'}, dimensions={0} | all-to-all | bytes 393216 | tf_op jit(solution)/shard_map/all_to_all | solution.py:572
  60.0 1.8 %shard_map.142 = (f32[128,256]{1,0:T(8,128)}, f32[3,128,256]{2,1,0:T(8,128)}, f32[8,256]{1,0:T(8,128)}) custom-call(bf16[768,128]{1,0:T(8,128)(2,1)S(1)} %bitcast.6, f32[3,128,256]{2,1,0:T(8,128)S(1)} %get-tuple-element.31.feat_ref, f32[3,128,896]{2,1,0:T(8,128)S(1)} %get-tuple-element.32.w_ref, f32[128,128]{1,0:T(8,128)S(1)} %get-tuple-element.33.skip_ref, ...), custom_call_target="tpu_custom_call" | custom-call | bytes 1048576 | tf_op jit(solution)/shard_map/pallas_call | solution.py:545
Async XLA Ops:
  32.9 0.7 %collective-permute-start = (bf16[320,128]{1,0:T(8,128)(2,1)S(1)}, bf16[320,128]{1,0:T(8,128)(2,1)S(1)}, u32[]{:S(2)}, u32[]{:S(2)}) collective-permute-start(bf16[320,128]{1,0:T(8,128)(2,1)S(1)} %get-tuple-element.28), channel_id=1, source_target_pairs={{0,0},{1,1},{2,2},{3,3},{4,4},{5,5},{6,6},{7,7},{8,8},{9,9},{10,10... | collective-permute-start | bytes 245768 | tf_op jit(solution)/shard_map/ppermute | solution.py:618

commit v6 on v5

--- a/solution.py
+++ b/solution.py
@@ -22,6 +22,7 @@
 IN_TOP_LANE = 16 * RIM
 TOP_LANE = 12 * RIM
 REACH = 125.0
+IN_FIRST, OUT_FIRST = 36, 36
 TABLES = 7
 CHUNK = 16
 
@@ -85,16 +86,23 @@
     return jnp.where(code < 0.0, -value, value)
 
 
+def turned_rows(value, first):
+    first %= value.shape[0]
+    return jnp.concatenate([value[first:], value[:first]], axis=0) if first else value
+
+
 class Lines:
-    def __init__(self, ref, rows):
+    def __init__(self, ref, rows, first=0):
         self.ref, self.rows = ref, rows
         self.count = ref.shape[0] // rows
+        self.first = first % self.count
 
     def get(self, row):
-        return self.ref[pl.ds(row, self.count, stride=self.rows), :]
+        value = self.ref[pl.ds(row, self.count, stride=self.rows), :]
+        return turned_rows(value, self.count - self.first)
 
     def put(self, row, value):
-        self.ref[pl.ds(row, self.count, stride=self.rows), :] = value
+        self.ref[pl.ds(row, self.count, stride=self.rows), :] = turned_rows(value, self.first)
 
     def get_block(self, row):
         return jnp.concatenate([self.get(row), self.get(row + 1)], axis=1)
@@ -204,7 +212,7 @@
     ]
     for copy in copies:
         copy.start()
-    lines = Lines(scratch, IN_ROWS)
+    lines = Lines(scratch, IN_ROWS, IN_FIRST)
     pieces = lines.count
     member = lax.axis_index("ch")
     position = lax.axis_index("ctx")
@@ -322,7 +330,7 @@
     cross_scratch,
 ):
     scratch[...] = r_ref[...].astype(F32)
-    lines = Lines(scratch, IN_ROWS)
+    lines = Lines(scratch, IN_ROWS, IN_FIRST)
     cross = Lines(cross_scratch, CROSS_ROWS)
     pieces = lines.count
     count = 2 * pieces
@@ -396,7 +404,7 @@
 ):
     cross_scratch[...] = cross_ref[...].astype(F32)
     cross = Lines(cross_scratch, CROSS_ROWS)
-    lines = Lines(scratch, OUT_ROWS)
+    lines = Lines(scratch, OUT_ROWS, OUT_FIRST)
     pieces = lines.count
     count = 2 * pieces
     length = 2 * LANES
@@ -462,7 +470,7 @@
 ):
     member = lax.axis_index("ch")
     scratch[...] = r_ref[...].astype(F32)
-    lines = Lines(scratch, OUT_ROWS)
+    lines = Lines(scratch, OUT_ROWS, OUT_FIRST)
     pieces = lines.count
     copies = []
 
@@ -567,9 +575,11 @@
     def room(rows):
         return pltpu.VMEM((pieces * rows, LANES), F32)
 
-    def transposed(array):
+    def transposed(array, first):
         rows = array.shape[0] // pieces
-        array = lax.all_to_all(array.reshape(pieces, rows // 2, 2, LANES), "ctx", 0, 0)
+        order = [(place + first) % pieces for place in range(pieces)]
+        array = array.reshape(pieces, rows // 2, 2, LANES)
+        array = lax.all_to_all(array, "ctx", 0, 0, axis_index_groups=[order])
         return array.reshape(pieces * rows, LANES)
 
     taps = jnp.transpose(short_weight, (0, 2, 1))
@@ -598,7 +608,7 @@
         ],
         specs={operand: HBM_SPEC for operand in range(5 + TABLES)},
     )
-    received = transposed(sent)
+    received = transposed(sent, IN_FIRST)
     cross, spectra, kept = call(
         forward_kernel,
         (
@@ -623,7 +633,7 @@
         [room(CROSS_ROWS), room(OUT_ROWS)],
         flops=800000000,
     )
-    received = transposed(sent)
+    received = transposed(sent, OUT_FIRST)
 
     return call(
         functools.partial(local_kernel, owners),

time: 62.3 us -> 57.8 us (0.928)
  blocking collectives: 53.7 us -> 49.5 us
    all_to_all x2, blocking collectives: 53.7 us -> 49.5 us  [transposed(): array = lax.all_to_all(array, 'ctx', 0, 0, axis_index_groups=[order])]
where the time goes in v6:
time: 57.8 us; the launch traced here: 57.6 us
  blocking collectives  49.5 us (86%)
  Pallas kernels  6.75 us (12%)
  starting transfers between devices  0.67 us (1%)
  between operations  0.67 us (1%)
    all_to_all x2, blocking collectives, transposed(): array = lax.all_to_all(array, 'ctx', 0, 0, axis_index_groups=[order])  49.5 us
    pallas_call x4, Pallas kernels, call(): pl.pallas_call(kernel, out_shape=out_shape, in_specs=[specs.get(place, VM...  6.75 us
  transfers between devices with their start and end apart: 1, of which 0 were waited for; matrix products, arithmetic and copies ran while one was open for 0% of the time, Pallas kernels for 0%

profile of v6, /device:TPU:1, one launch (start us, length us, event | category | flops | bytes accessed | tf_op | source)
XLA Modules:
  0.0 57.6 jit_solution(2703149206198541218)
XLA Ops:
  0.6 2.1 %shard_map.139 = (bf16[768,128]{1,0:T(8,128)(2,1)S(1)}, f32[8,128]{1,0:T(8,128)S(1)}, f32[3,128,256]{2,1,0:T(8,128)S(1)}, f32[3,128,896]{2,1,0:T(8,128)S(1)}, f3...) custom-call(bf16[3,128,256]{2,1,0:T(8,128)(2,1)} %refs_0_.1, ...), custom_call_target="tpu_custom_call" | custom-call | bytes 1048576 | tf_op jit(solution)/shard_map/pallas_call | solution.py:553
  2.7 24.0 %all_to_all.10 = bf16[64,6,2,128]{3,2,1,0:T(2,128)(2,1)S(1)} all-to-all(bf16[64,6,2,128]{3,2,1,0:T(2,128)(2,1)S(1)} %bitcast.7), channel_id=1, replica_groups={{288,296,304,312,320,328,336,344,352,360,368,376,384,392,400,408,416,42..., dimensions={0} | all-to-all | bytes 393216 | tf_op jit(solution)/shard_map/all_to_all | solution.py:582
  26.7 1.5 %shard_map.140 = (bf16[320,128]{1,0:T(8,128)(2,1)S(1)}, f32[512,256]{1,0:T(8,128)S(1)}, f32[6,64,128]{2,1,0:T(8,128)S(1)}) custom-call(bf16[768,128]{1,0:T(8,128)(2,1)S(1)} %bitcast.9, f32[8,128]{1,0:T(8,128)S(1)} %get-tuple-element.20.w_ref, bf16[256,128]{1,0:T(8,128)(2,1)S(1)} %get-tuple-element.21.outer_hi, ...), custom_call_target="tpu_custom_call" | custom-call | flops 800000000 | bytes 1048576 | tf_op jit(solution)/shard_map/pallas_call | solution.py:553
  28.2 0.7 %collective-permute-start = (bf16[320,128]{1,0:T(8,128)(2,1)S(1)}, bf16[320,128]{1,0:T(8,128)(2,1)S(1)}, u32[]{:S(2)}, u32[]{:S(2)}) collective-permute-start(bf16[320,128]{1,0:T(8,128)(2,1)S(1)} %get-tuple-element.28), channel_id=1, source_target_pairs={{0,0},{1,1},{2,2},{3,3},{4,4},{5,5},{6,6},{7,7},{8,8},{9,9},{10,10... | collective-permute-start | bytes 245768 | tf_op jit(solution)/shard_map/ppermute | solution.py:628
  28.9 0.0 collective-permute-done.cross_ref
  28.9 1.4 %shard_map.141 = bf16[768,128]{1,0:T(8,128)(2,1)S(1)} custom-call(bf16[320,128]{1,0:T(8,128)(2,1)S(1)} %collective-permute-done.cross_ref, f32[512,256]{1,0:T(8,128)S(1)} %get-tuple-element.29.spec_ref, f32[6,64,128]{2,1,0:T(8,128)S(1)} %get-tuple-element.30.kept_ref, f32[8,128]{1,0:T(8,128)S(1)} %get-tuple-element.20.w_ref, ...), custom_call_target="tpu_custom_call" | custom-call | flops 800000000 | bytes 1048576 | tf_op jit(solution)/shard_map/pallas_call | solution.py:553
  30.3 25.5 %all_to_all.11 = bf16[64,6,2,128]{3,2,1,0:T(2,128)(2,1)S(1)} all-to-all(bf16[64,6,2,128]{3,2,1,0:T(2,128)(2,1)S(1)} %bitcast.8), channel_id=1, replica_groups={{288,296,304,312,320,328,336,344,352,360,368,376,384,392,400,408,416,42..., dimensions={0} | all-to-all | bytes 393216 | tf_op jit(solution)/shard_map/all_to_all | solution.py:582
  55.8 1.8 %shard_map.142 = (f32[128,256]{1,0:T(8,128)}, f32[3,128,256]{2,1,0:T(8,128)}, f32[8,256]{1,0:T(8,128)}) custom-call(bf16[768,128]{1,0:T(8,128)(2,1)S(1)} %bitcast.6, f32[3,128,256]{2,1,0:T(8,128)S(1)} %get-tuple-element.31.feat_ref, f32[3,128,896]{2,1,0:T(8,128)S(1)} %get-tuple-element.32.w_ref, f32[128,128]{1,0:T(8,128)S(1)} %get-tuple-element.33.skip_ref, ...), custom_call_target="tpu_custom_call" | custom-call | bytes 1048576 | tf_op jit(solution)/shard_map/pallas_call | solution.py:553
Async XLA Ops:
  28.2 0.7 %collective-permute-start = (bf16[320,128]{1,0:T(8,128)(2,1)S(1)}, bf16[320,128]{1,0:T(8,128)(2,1)S(1)}, u32[]{:S(2)}, u32[]{:S(2)}) collective-permute-start(bf16[320,128]{1,0:T(8,128)(2,1)S(1)} %get-tuple-element.28), channel_id=1, source_target_pairs={{0,0},{1,1},{2,2},{3,3},{4,4},{5,5},{6,6},{7,7},{8,8},{9,9},{10,10... | collective-permute-start | bytes 245768 | tf_op jit(solution)/shard_map/ppermute | solution.py:628

commit v7 on v6

--- a/solution.py
+++ b/solution.py
@@ -22,7 +22,7 @@
 IN_TOP_LANE = 16 * RIM
 TOP_LANE = 12 * RIM
 REACH = 125.0
-IN_FIRST, OUT_FIRST = 36, 36
+IN_FIRST, OUT_FIRST = 44, 44
 TABLES = 7
 CHUNK = 16
 

time: 57.8 us -> 57.5 us (level)
  no operation moved by 1% of the time
where the time goes in v7:
time: 57.5 us; the launch traced here: 57.2 us
  blocking collectives  49.1 us (85%)
  Pallas kernels  6.75 us (12%)
  starting transfers between devices  0.67 us (1%)
  between operations  0.67 us (1%)
    all_to_all x2, blocking collectives, transposed(): array = lax.all_to_all(array, 'ctx', 0, 0, axis_index_groups=[order])  49.1 us
    pallas_call x4, Pallas kernels, call(): pl.pallas_call(kernel, out_shape=out_shape, in_specs=[specs.get(place, VM...  6.75 us
  transfers between devices with their start and end apart: 1, of which 0 were waited for; matrix products, arithmetic and copies ran while one was open for 0% of the time, Pallas kernels for 0%

profile of v7, /device:TPU:1, one launch (start us, length us, event | category | flops | bytes accessed | tf_op | source)
XLA Modules:
  0.0 57.2 jit_solution(15011253922257671049)
XLA Ops:
  0.6 2.1 %shard_map.139 = (bf16[768,128]{1,0:T(8,128)(2,1)S(1)}, f32[8,128]{1,0:T(8,128)S(1)}, f32[3,128,256]{2,1,0:T(8,128)S(1)}, f32[3,128,896]{2,1,0:T(8,128)S(1)}, f3...) custom-call(bf16[3,128,256]{2,1,0:T(8,128)(2,1)} %refs_0_.1, ...), custom_call_target="tpu_custom_call" | custom-call | bytes 1048576 | tf_op jit(solution)/shard_map/pallas_call | solution.py:553
  2.7 24.0 %all_to_all.10 = bf16[64,6,2,128]{3,2,1,0:T(2,128)(2,1)S(1)} all-to-all(bf16[64,6,2,128]{3,2,1,0:T(2,128)(2,1)S(1)} %bitcast.7), channel_id=1, replica_groups={{352,360,368,376,384,392,400,408,416,424,432,440,448,456,464,472,480,48..., dimensions={0} | all-to-all | bytes 393216 | tf_op jit(solution)/shard_map/all_to_all | solution.py:582
  26.7 1.5 %shard_map.140 = (bf16[320,128]{1,0:T(8,128)(2,1)S(1)}, f32[512,256]{1,0:T(8,128)S(1)}, f32[6,64,128]{2,1,0:T(8,128)S(1)}) custom-call(bf16[768,128]{1,0:T(8,128)(2,1)S(1)} %bitcast.9, f32[8,128]{1,0:T(8,128)S(1)} %get-tuple-element.20.w_ref, bf16[256,128]{1,0:T(8,128)(2,1)S(1)} %get-tuple-element.21.outer_hi, ...), custom_call_target="tpu_custom_call" | custom-call | flops 800000000 | bytes 1048576 | tf_op jit(solution)/shard_map/pallas_call | solution.py:553
  28.2 0.7 %collective-permute-start = (bf16[320,128]{1,0:T(8,128)(2,1)S(1)}, bf16[320,128]{1,0:T(8,128)(2,1)S(1)}, u32[]{:S(2)}, u32[]{:S(2)}) collective-permute-start(bf16[320,128]{1,0:T(8,128)(2,1)S(1)} %get-tuple-element.28), channel_id=1, source_target_pairs={{0,0},{1,1},{2,2},{3,3},{4,4},{5,5},{6,6},{7,7},{8,8},{9,9},{10,10... | collective-permute-start | bytes 245768 | tf_op jit(solution)/shard_map/ppermute | solution.py:628
  28.9 0.0 collective-permute-done.cross_ref
  28.9 1.4 %shard_map.141 = bf16[768,128]{1,0:T(8,128)(2,1)S(1)} custom-call(bf16[320,128]{1,0:T(8,128)(2,1)S(1)} %collective-permute-done.cross_ref, f32[512,256]{1,0:T(8,128)S(1)} %get-tuple-element.29.spec_ref, f32[6,64,128]{2,1,0:T(8,128)S(1)} %get-tuple-element.30.kept_ref, f32[8,128]{1,0:T(8,128)S(1)} %get-tuple-element.20.w_ref, ...), custom_call_target="tpu_custom_call" | custom-call | flops 800000000 | bytes 1048576 | tf_op jit(solution)/shard_map/pallas_call | solution.py:553
  30.3 25.1 %all_to_all.11 = bf16[64,6,2,128]{3,2,1,0:T(2,128)(2,1)S(1)} all-to-all(bf16[64,6,2,128]{3,2,1,0:T(2,128)(2,1)S(1)} %bitcast.8), channel_id=1, replica_groups={{352,360,368,376,384,392,400,408,416,424,432,440,448,456,464,472,480,48..., dimensions={0} | all-to-all | bytes 393216 | tf_op jit(solution)/shard_map/all_to_all | solution.py:582
  55.4 1.8 %shard_map.142 = (f32[128,256]{1,0:T(8,128)}, f32[3,128,256]{2,1,0:T(8,128)}, f32[8,256]{1,0:T(8,128)}) custom-call(bf16[768,128]{1,0:T(8,128)(2,1)S(1)} %bitcast.6, f32[3,128,256]{2,1,0:T(8,128)S(1)} %get-tuple-element.31.feat_ref, f32[3,128,896]{2,1,0:T(8,128)S(1)} %get-tuple-element.32.w_ref, f32[128,128]{1,0:T(8,128)S(1)} %get-tuple-element.33.skip_ref, ...), custom_call_target="tpu_custom_call" | custom-call | bytes 1048576 | tf_op jit(solution)/shard_map/pallas_call | solution.py:553
Async XLA Ops:
  28.2 0.7 %collective-permute-start = (bf16[320,128]{1,0:T(8,128)(2,1)S(1)}, bf16[320,128]{1,0:T(8,128)(2,1)S(1)}, u32[]{:S(2)}, u32[]{:S(2)}) collective-permute-start(bf16[320,128]{1,0:T(8,128)(2,1)S(1)} %get-tuple-element.28), channel_id=1, source_target_pairs={{0,0},{1,1},{2,2},{3,3},{4,4},{5,5},{6,6},{7,7},{8,8},{9,9},{10,10... | collective-permute-start | bytes 245768 | tf_op jit(solution)/shard_map/ppermute | solution.py:628

commit v8 on v7

--- a/solution.py
+++ b/solution.py
@@ -22,7 +22,7 @@
 IN_TOP_LANE = 16 * RIM
 TOP_LANE = 12 * RIM
 REACH = 125.0
-IN_FIRST, OUT_FIRST = 44, 44
+IN_FIRST, OUT_FIRST = 45, 45
 TABLES = 7
 CHUNK = 16
 

time: 57.5 us -> 57.4 us (level)
  no operation moved by 1% of the time
where the time goes in v8:
time: 57.4 us; the launch traced here: 57.2 us
  blocking collectives  49.1 us (86%)
  Pallas kernels  6.75 us (12%)
  starting transfers between devices  0.67 us (1%)
  between operations  0.67 us (1%)
    all_to_all x2, blocking collectives, transposed(): array = lax.all_to_all(array, 'ctx', 0, 0, axis_index_groups=[order])  49.1 us
    pallas_call x4, Pallas kernels, call(): pl.pallas_call(kernel, out_shape=out_shape, in_specs=[specs.get(place, VM...  6.75 us
  transfers between devices with their start and end apart: 1, of which 0 were waited for; matrix products, arithmetic and copies ran while one was open for 0% of the time, Pallas kernels for 0%

profile of v8, /device:TPU:1, one launch (start us, length us, event | category | flops | bytes accessed | tf_op | source)
XLA Modules:
  0.0 57.2 jit_solution(1912117701841687104)
XLA Ops:
  0.6 2.1 %shard_map.139 = (bf16[768,128]{1,0:T(8,128)(2,1)S(1)}, f32[8,128]{1,0:T(8,128)S(1)}, f32[3,128,256]{2,1,0:T(8,128)S(1)}, f32[3,128,896]{2,1,0:T(8,128)S(1)}, f3...) custom-call(bf16[3,128,256]{2,1,0:T(8,128)(2,1)} %refs_0_.1, ...), custom_call_target="tpu_custom_call" | custom-call | bytes 1048576 | tf_op jit(solution)/shard_map/pallas_call | solution.py:553
  2.7 24.0 %all_to_all.10 = bf16[64,6,2,128]{3,2,1,0:T(2,128)(2,1)S(1)} all-to-all(bf16[64,6,2,128]{3,2,1,0:T(2,128)(2,1)S(1)} %bitcast.7), channel_id=1, replica_groups={{360,368,376,384,392,400,408,416,424,432,440,448,456,464,472,480,488,49..., dimensions={0} | all-to-all | bytes 393216 | tf_op jit(solution)/shard_map/all_to_all | solution.py:582
  26.7 1.5 %shard_map.140 = (bf16[320,128]{1,0:T(8,128)(2,1)S(1)}, f32[512,256]{1,0:T(8,128)S(1)}, f32[6,64,128]{2,1,0:T(8,128)S(1)}) custom-call(bf16[768,128]{1,0:T(8,128)(2,1)S(1)} %bitcast.9, f32[8,128]{1,0:T(8,128)S(1)} %get-tuple-element.20.w_ref, bf16[256,128]{1,0:T(8,128)(2,1)S(1)} %get-tuple-element.21.outer_hi, ...), custom_call_target="tpu_custom_call" | custom-call | flops 800000000 | bytes 1048576 | tf_op jit(solution)/shard_map/pallas_call | solution.py:553
  28.2 0.7 %collective-permute-start = (bf16[320,128]{1,0:T(8,128)(2,1)S(1)}, bf16[320,128]{1,0:T(8,128)(2,1)S(1)}, u32[]{:S(2)}, u32[]{:S(2)}) collective-permute-start(bf16[320,128]{1,0:T(8,128)(2,1)S(1)} %get-tuple-element.28), channel_id=1, source_target_pairs={{0,0},{1,1},{2,2},{3,3},{4,4},{5,5},{6,6},{7,7},{8,8},{9,9},{10,10... | collective-permute-start | bytes 245768 | tf_op jit(solution)/shard_map/ppermute | solution.py:628
  28.9 0.0 collective-permute-done.cross_ref
  28.9 1.4 %shard_map.141 = bf16[768,128]{1,0:T(8,128)(2,1)S(1)} custom-call(bf16[320,128]{1,0:T(8,128)(2,1)S(1)} %collective-permute-done.cross_ref, f32[512,256]{1,0:T(8,128)S(1)} %get-tuple-element.29.spec_ref, f32[6,64,128]{2,1,0:T(8,128)S(1)} %get-tuple-element.30.kept_ref, f32[8,128]{1,0:T(8,128)S(1)} %get-tuple-element.20.w_ref, ...), custom_call_target="tpu_custom_call" | custom-call | flops 800000000 | bytes 1048576 | tf_op jit(solution)/shard_map/pallas_call | solution.py:553
  30.3 25.1 %all_to_all.11 = bf16[64,6,2,128]{3,2,1,0:T(2,128)(2,1)S(1)} all-to-all(bf16[64,6,2,128]{3,2,1,0:T(2,128)(2,1)S(1)} %bitcast.8), channel_id=1, replica_groups={{360,368,376,384,392,400,408,416,424,432,440,448,456,464,472,480,488,49..., dimensions={0} | all-to-all | bytes 393216 | tf_op jit(solution)/shard_map/all_to_all | solution.py:582
  55.5 1.8 %shard_map.142 = (f32[128,256]{1,0:T(8,128)}, f32[3,128,256]{2,1,0:T(8,128)}, f32[8,256]{1,0:T(8,128)}) custom-call(bf16[768,128]{1,0:T(8,128)(2,1)S(1)} %bitcast.6, f32[3,128,256]{2,1,0:T(8,128)S(1)} %get-tuple-element.31.feat_ref, f32[3,128,896]{2,1,0:T(8,128)S(1)} %get-tuple-element.32.w_ref, f32[128,128]{1,0:T(8,128)S(1)} %get-tuple-element.33.skip_ref, ...), custom_call_target="tpu_custom_call" | custom-call | bytes 1048576 | tf_op jit(solution)/shard_map/pallas_call | solution.py:553
Async XLA Ops:
  28.2 0.7 %collective-permute-start = (bf16[320,128]{1,0:T(8,128)(2,1)S(1)}, bf16[320,128]{1,0:T(8,128)(2,1)S(1)}, u32[]{:S(2)}, u32[]{:S(2)}) collective-permute-start(bf16[320,128]{1,0:T(8,128)(2,1)S(1)} %get-tuple-element.28), channel_id=1, source_target_pairs={{0,0},{1,1},{2,2},{3,3},{4,4},{5,5},{6,6},{7,7},{8,8},{9,9},{10,10... | collective-permute-start | bytes 245768 | tf_op jit(solution)/shard_map/ppermute | solution.py:628
